TPU v7x, 256 devices: a whole 4x4x8 slice. The times are simulated.
256 devices in a mesh: seq: 32 (over y_hi, z, core), head: 8 (over y_lo, x).
Axes of the slice: x: 4, y: 4 (y_hi: 2, y_lo: 2; y = y_hi * 2 + y_lo), z: 8, core: 2. Of those that a mesh axis runs over, the one named last changes fastest.
Arguments:
- queries: bfloat16 [4096, 2048], P('seq', 'head'), may hold values from -6 to 6
- keys: bfloat16 [4096, 2048], P('seq', 'head'), may hold values from -6 to 6
- values: bfloat16 [4096, 2048], P('seq', 'head'), may hold values from -6 to 6
- attn_out: bfloat16 [4096, 2048], P('seq', 'head'), may hold values from -6 to 6
- out_grad: bfloat16 [4096, 4096], P('seq', 'head'), may hold values from -6 to 6
- out_weight: bfloat16 [2048, 4096], P('head'), may hold values from -0.125 to 0.125
- segment_ids: int32 [4096], replicated, may hold values from 0 to 3, as said below
Outputs:
- query_grad: bfloat16 [4096, 2048], P('seq', 'head')
- key_grad: bfloat16 [4096, 2048], P('seq', 'head')
- value_grad: bfloat16 [4096, 2048], P('seq', 'head')
Inputs may be any that keep to these rules, and one draw needn't show every extreme that they name: `segment_ids`: ids 0 to 3 never falling along the tokens; each of the 4 documents starts at a multiple of 16 tokens, and one of them is exactly 3072 tokens long.
All inputs are finite; a program needn't handle non-finite values.
Results may differ from a plain program's by a relative error of at most 0.0058.
Values may be sent and summed in bfloat16 or wider, within the bound.
A program may use at most 64 MiB of HBM per device.

v0:
```python
import jax
import jax.numpy as jnp
from jax import lax
from jax.sharding import PartitionSpec as P

HD = 128


def shifted(block, axis, distance):
    devices = range(lax.axis_size(axis))
    route = [((i - distance) % len(devices), i) for i in devices]
    return lax.ppermute(block, axis, route)


def head_view(array, heads):
    return array.reshape(array.shape[0], heads, HD)


def tile_grads(
    query_part,
    grad_part,
    log_part,
    delta_part,
    query_segments,
    key_part,
    value_part,
    key_segments,
    scaling,
):
    scores = (
        jnp.einsum("qhd,khd->hqk", query_part, key_part, preferred_element_type=jnp.float32)
        * scaling
    )
    allowed = (query_segments[:, None] == key_segments[None, :])[None]
    lowered = jnp.where(allowed, scores, log_part[..., None]) - log_part[..., None]
    probs = jnp.where(allowed, jnp.exp(lowered), 0.0)
    prob_grad = jnp.einsum(
        "qhd,khd->hqk", grad_part, value_part, preferred_element_type=jnp.float32
    )
    score_grad = probs * (prob_grad - delta_part[..., None])
    probs_low = probs.astype(jnp.bfloat16)
    score_low = (score_grad * scaling).astype(jnp.bfloat16)
    value_add = jnp.einsum("hqk,qhd->khd", probs_low, grad_part, preferred_element_type=jnp.float32)
    key_add = jnp.einsum("hqk,qhd->khd", score_low, query_part, preferred_element_type=jnp.float32)
    query_add = jnp.einsum("hqk,khd->qhd", score_low, key_part, preferred_element_type=jnp.float32)
    return (key_add, value_add, query_add)


def stats_core(carried, query_heads, query_segments, key_part, key_segments, scaling):
    largest, summed = carried
    scores = (
        jnp.einsum("qhd,khd->hqk", query_heads, key_part, preferred_element_type=jnp.float32)
        * scaling
    )
    allowed = (query_segments[:, None] == key_segments[None, :])[None]
    newest = jnp.maximum(largest, jnp.max(jnp.where(allowed, scores, -1e30), axis=-1))
    centred = jnp.where(allowed, scores, newest[..., None]) - newest[..., None]
    summed = jnp.sum(jnp.where(allowed, jnp.exp(centred), 0.0), axis=-1)
    return (newest, summed)


def cycle_pass(
    query_heads,
    grad_heads,
    log_sums,
    deltas,
    query_segments,
    key_heads,
    value_heads,
    segment_ids,
    scaling,
    groups,
):
    cycle_size = lax.axis_size("seq")
    cycle_place = lax.axis_index("seq")
    tok_rows = query_heads.shape[0]

    def advance(blocks, grad_pairs, query_total, turn_index, shift_blocks):
        new_blocks = []
        new_grads = []
        query_parts = []
        for member, (first_head, last_head, direction_sign, move_blocks, move_grads) in enumerate(
            groups
        ):
            key_part, value_part = blocks[member]
            anchor = (cycle_place - direction_sign * turn_index) % cycle_size
            key_segments = lax.dynamic_slice_in_dim(segment_ids, anchor * tok_rows, tok_rows)
            key_add, value_add, query_add = tile_grads(
                query_heads,
                grad_heads,
                log_sums,
                deltas,
                query_segments,
                key_part,
                value_part,
                key_segments,
                scaling,
            )
            query_parts.append(query_add)
            new_grads.append(
                tuple(
                    move_grads(grad_pairs[member][0] + key_add, grad_pairs[member][1] + value_add)
                )
            )
            if shift_blocks:
                new_blocks.append(tuple(move_blocks(key_part, value_part)))
            else:
                new_blocks.append((key_part, value_part))
        return (new_blocks, new_grads, query_total + jnp.concatenate(query_parts, axis=1))

    def cycle_turn(turn_index, carried):
        return advance(carried[0], carried[1], carried[2], turn_index, True)

    start_blocks = []
    start_grads = []
    for first_head, last_head, direction_sign, move_blocks, move_grads in groups:
        start_blocks.append((key_heads, value_heads))
        blank = jnp.zeros((tok_rows, last_head - first_head, HD), jnp.float32)
        start_grads.append((blank, blank))
    query_start = jnp.zeros(query_heads.shape, jnp.float32)
    carried = lax.fori_loop(0, cycle_size - 1, cycle_turn, (start_blocks, start_grads, query_start))
    finished = advance(carried[0], carried[1], carried[2], cycle_size - 1, False)
    key_total = jnp.concatenate([pair[0] for pair in finished[1]], axis=1)
    value_total = jnp.concatenate([pair[1] for pair in finished[1]], axis=1)
    return (finished[2], key_total, value_total)


def shards(queries, keys, values, attn_out, out_grad, out_weight, segment_ids):
    scaling = HD ** (-0.5)
    tok_rows = queries.shape[0]
    local_heads = queries.shape[1] // HD
    cycle_place = lax.axis_index("seq")
    query_segments = lax.dynamic_slice_in_dim(segment_ids, cycle_place * tok_rows, tok_rows)
    grad_attn = lax.dot_general(
        lax.all_gather(out_grad, "head", axis=1, tiled=True),
        out_weight,
        (((1,), (1,)), ((), ())),
        preferred_element_type=jnp.float32,
    ).astype(jnp.bfloat16)
    query_heads = head_view(queries, local_heads)
    key_heads = head_view(keys, local_heads)
    value_heads = head_view(values, local_heads)
    grad_heads = head_view(grad_attn, local_heads)
    out_heads = head_view(attn_out, local_heads)
    deltas = jnp.sum(grad_heads.astype(jnp.float32) * out_heads.astype(jnp.float32), axis=-1).T
    stats_start = (
        jnp.full((local_heads, tok_rows), -1e30, jnp.float32),
        jnp.zeros((local_heads, tok_rows), jnp.float32),
    )
    largest, summed = stats_core(
        stats_start,
        query_heads,
        query_segments,
        head_view(lax.all_gather(keys, "seq", axis=0, tiled=True), local_heads),
        segment_ids,
        scaling,
    )
    log_sums = largest + jnp.log(summed)

    def blocks_ahead(key_part, value_part):
        return shifted((key_part, value_part), "seq", 1)

    def grads_ahead(key_part, value_part):
        return shifted((key_part, value_part), "seq", 1)

    groups = [(0, local_heads, 1, blocks_ahead, grads_ahead)]
    query_total, key_total, value_total = cycle_pass(
        query_heads,
        grad_heads,
        log_sums,
        deltas,
        query_segments,
        key_heads,
        value_heads,
        segment_ids,
        scaling,
        groups,
    )
    return (
        query_total.astype(jnp.bfloat16).reshape(tok_rows, -1),
        key_total.astype(jnp.bfloat16).reshape(tok_rows, -1),
        value_total.astype(jnp.bfloat16).reshape(tok_rows, -1),
    )


def solution(mesh):
    return jax.shard_map(
        shards,
        mesh=mesh,
        in_specs=(
            P("seq", "head"),
            P("seq", "head"),
            P("seq", "head"),
            P("seq", "head"),
            P("seq", "head"),
            P("head", None),
            P(),
        ),
        out_specs=(P("seq", "head"), P("seq", "head"), P("seq", "head")),
        check_vma=False,
    )
```

profile of v0, /device:TPU:1, one launch (start us, length us, event | category | flops | bytes accessed | tf_op | source)
XLA Modules:
  0.0 494.2 jit_solution(14696772495360528847)
XLA Ops:
  15.7 34.4 %all-gather.5.cloned.1.call-done = bf16[128,4096]{1,0:T(8,128)(2,1)} async-done(((bf16[128,512]{1,0:T(8,128)(2,1)}), bf16[128,4096]{1,0:T(8,128)(2,1)}) %all-gather.5.cloned.1.call-update) | async-done | bytes 1048592 | tf_op jit(solution)/shard_map/all_gather | solution.py:135
  50.0 2.1 convolution_convert_fusion
  52.4 82.7 %all-gather.3.cloned.1.call-done = bf16[4096,256]{0,1:T(8,128)(2,1)} async-done(((bf16[128,256]{0,1:T(8,128)(2,1)}), bf16[4096,256]{0,1:T(8,128)(2,1)}) %all-gather.3.cloned.1.call-update) | async-done | bytes 2097168 | tf_op jit(solution)/shard_map/all_gather | solution.py:154
  135.1 2.9 select_reduce_fusion.1
  139.3 336.8 %while.24 = (s32[]{:T(128)}, bf16[128,2,128]{2,0,1:T(8,128)(2,1)S(1)}, bf16[128,2,128]{2,0,1:T(8,128)(2,1)S(1)}, f32[128,2,128]{2,0,1:T(8,128)S(1)}, f32[128,2,1...) while((s32[]{:T(128)}, ...), condition=%wide.region_4.5_spmd.clone, body=%wide.region_3.4_spmd.clone.sunk | while | flops 42385424 | bytes 3707394 | solution.py:121
  146.0 2.5 collective-permute-start
  150.0 1.8 collective-permute-start.2
  152.8 1.7 collective-permute-done.2
  155.1 2.5 collective-permute-start
  160.8 3.0 collective-permute-done
  163.9 1.7 collective-permute-done.2
  167.6 2.5 collective-permute-start.2
  170.6 4.2 collective-permute-done
  174.9 1.7 collective-permute-done.2
  179.4 6.5 %collective-permute-done = bf16[128,2,128]{2,0,1:T(8,128)(2,1)S(1)} collective-permute-done((bf16[128,2,128]{2,0,1:T(8,128)(2,1)S(1)}, bf16[128,2,128]{2,0,1:T(8,128)(2,1)S(1)}, u32[]{:S(2)}, u32[]{:S(2)}) %collective-permute-start) | collective-permute-done | bytes 65568 | tf_op jit(solution)/shard_map/while/body/eval_jaxpr/ppermute | solution.py:12
  186.0 1.7 collective-permute-done.2
  190.2 6.8 %collective-permute-done = bf16[128,2,128]{2,0,1:T(8,128)(2,1)S(1)} collective-permute-done((bf16[128,2,128]{2,0,1:T(8,128)(2,1)S(1)}, bf16[128,2,128]{2,0,1:T(8,128)(2,1)S(1)}, u32[]{:S(2)}, u32[]{:S(2)}) %collective-permute-start) | collective-permute-done | bytes 65568 | tf_op jit(solution)/shard_map/while/body/eval_jaxpr/ppermute | solution.py:12
  197.1 1.7 collective-permute-done.2
  201.3 6.8 %collective-permute-done = bf16[128,2,128]{2,0,1:T(8,128)(2,1)S(1)} collective-permute-done((bf16[128,2,128]{2,0,1:T(8,128)(2,1)S(1)}, bf16[128,2,128]{2,0,1:T(8,128)(2,1)S(1)}, u32[]{:S(2)}, u32[]{:S(2)}) %collective-permute-start) | collective-permute-done | bytes 65568 | tf_op jit(solution)/shard_map/while/body/eval_jaxpr/ppermute | solution.py:12
  208.2 1.7 collective-permute-done.2
  212.4 6.8 %collective-permute-done = bf16[128,2,128]{2,0,1:T(8,128)(2,1)S(1)} collective-permute-done((bf16[128,2,128]{2,0,1:T(8,128)(2,1)S(1)}, bf16[128,2,128]{2,0,1:T(8,128)(2,1)S(1)}, u32[]{:S(2)}, u32[]{:S(2)}) %collective-permute-start) | collective-permute-done | bytes 65568 | tf_op jit(solution)/shard_map/while/body/eval_jaxpr/ppermute | solution.py:12
  219.3 1.7 collective-permute-done.2
  223.4 6.8 %collective-permute-done = bf16[128,2,128]{2,0,1:T(8,128)(2,1)S(1)} collective-permute-done((bf16[128,2,128]{2,0,1:T(8,128)(2,1)S(1)}, bf16[128,2,128]{2,0,1:T(8,128)(2,1)S(1)}, u32[]{:S(2)}, u32[]{:S(2)}) %collective-permute-start) | collective-permute-done | bytes 65568 | tf_op jit(solution)/shard_map/while/body/eval_jaxpr/ppermute | solution.py:12
  230.4 1.7 collective-permute-done.2
  234.5 6.8 %collective-permute-done = bf16[128,2,128]{2,0,1:T(8,128)(2,1)S(1)} collective-permute-done((bf16[128,2,128]{2,0,1:T(8,128)(2,1)S(1)}, bf16[128,2,128]{2,0,1:T(8,128)(2,1)S(1)}, u32[]{:S(2)}, u32[]{:S(2)}) %collective-permute-start) | collective-permute-done | bytes 65568 | tf_op jit(solution)/shard_map/while/body/eval_jaxpr/ppermute | solution.py:12
  241.4 1.7 collective-permute-done.2
  245.6 6.8 %collective-permute-done = bf16[128,2,128]{2,0,1:T(8,128)(2,1)S(1)} collective-permute-done((bf16[128,2,128]{2,0,1:T(8,128)(2,1)S(1)}, bf16[128,2,128]{2,0,1:T(8,128)(2,1)S(1)}, u32[]{:S(2)}, u32[]{:S(2)}) %collective-permute-start) | collective-permute-done | bytes 65568 | tf_op jit(solution)/shard_map/while/body/eval_jaxpr/ppermute | solution.py:12
  252.5 1.7 collective-permute-done.2
  256.7 6.8 %collective-permute-done = bf16[128,2,128]{2,0,1:T(8,128)(2,1)S(1)} collective-permute-done((bf16[128,2,128]{2,0,1:T(8,128)(2,1)S(1)}, bf16[128,2,128]{2,0,1:T(8,128)(2,1)S(1)}, u32[]{:S(2)}, u32[]{:S(2)}) %collective-permute-start) | collective-permute-done | bytes 65568 | tf_op jit(solution)/shard_map/while/body/eval_jaxpr/ppermute | solution.py:12
  263.6 1.7 collective-permute-done.2
  267.8 6.8 %collective-permute-done = bf16[128,2,128]{2,0,1:T(8,128)(2,1)S(1)} collective-permute-done((bf16[128,2,128]{2,0,1:T(8,128)(2,1)S(1)}, bf16[128,2,128]{2,0,1:T(8,128)(2,1)S(1)}, u32[]{:S(2)}, u32[]{:S(2)}) %collective-permute-start) | collective-permute-done | bytes 65568 | tf_op jit(solution)/shard_map/while/body/eval_jaxpr/ppermute | solution.py:12
  274.7 1.7 collective-permute-done.2
  278.8 6.8 %collective-permute-done = bf16[128,2,128]{2,0,1:T(8,128)(2,1)S(1)} collective-permute-done((bf16[128,2,128]{2,0,1:T(8,128)(2,1)S(1)}, bf16[128,2,128]{2,0,1:T(8,128)(2,1)S(1)}, u32[]{:S(2)}, u32[]{:S(2)}) %collective-permute-start) | collective-permute-done | bytes 65568 | tf_op jit(solution)/shard_map/while/body/eval_jaxpr/ppermute | solution.py:12
  285.8 1.7 collective-permute-done.2
  289.9 6.8 %collective-permute-done = bf16[128,2,128]{2,0,1:T(8,128)(2,1)S(1)} collective-permute-done((bf16[128,2,128]{2,0,1:T(8,128)(2,1)S(1)}, bf16[128,2,128]{2,0,1:T(8,128)(2,1)S(1)}, u32[]{:S(2)}, u32[]{:S(2)}) %collective-permute-start) | collective-permute-done | bytes 65568 | tf_op jit(solution)/shard_map/while/body/eval_jaxpr/ppermute | solution.py:12
  296.9 1.7 collective-permute-done.2
  301.0 6.8 %collective-permute-done = bf16[128,2,128]{2,0,1:T(8,128)(2,1)S(1)} collective-permute-done((bf16[128,2,128]{2,0,1:T(8,128)(2,1)S(1)}, bf16[128,2,128]{2,0,1:T(8,128)(2,1)S(1)}, u32[]{:S(2)}, u32[]{:S(2)}) %collective-permute-start) | collective-permute-done | bytes 65568 | tf_op jit(solution)/shard_map/while/body/eval_jaxpr/ppermute | solution.py:12
  307.9 1.7 collective-permute-done.2
  312.1 6.8 %collective-permute-done = bf16[128,2,128]{2,0,1:T(8,128)(2,1)S(1)} collective-permute-done((bf16[128,2,128]{2,0,1:T(8,128)(2,1)S(1)}, bf16[128,2,128]{2,0,1:T(8,128)(2,1)S(1)}, u32[]{:S(2)}, u32[]{:S(2)}) %collective-permute-start) | collective-permute-done | bytes 65568 | tf_op jit(solution)/shard_map/while/body/eval_jaxpr/ppermute | solution.py:12
  319.0 1.7 collective-permute-done.2
  323.2 6.8 %collective-permute-done = bf16[128,2,128]{2,0,1:T(8,128)(2,1)S(1)} collective-permute-done((bf16[128,2,128]{2,0,1:T(8,128)(2,1)S(1)}, bf16[128,2,128]{2,0,1:T(8,128)(2,1)S(1)}, u32[]{:S(2)}, u32[]{:S(2)}) %collective-permute-start) | collective-permute-done | bytes 65568 | tf_op jit(solution)/shard_map/while/body/eval_jaxpr/ppermute | solution.py:12
  330.1 1.7 collective-permute-done.2
  334.3 6.8 %collective-permute-done = bf16[128,2,128]{2,0,1:T(8,128)(2,1)S(1)} collective-permute-done((bf16[128,2,128]{2,0,1:T(8,128)(2,1)S(1)}, bf16[128,2,128]{2,0,1:T(8,128)(2,1)S(1)}, u32[]{:S(2)}, u32[]{:S(2)}) %collective-permute-start) | collective-permute-done | bytes 65568 | tf_op jit(solution)/shard_map/while/body/eval_jaxpr/ppermute | solution.py:12
  341.2 1.7 collective-permute-done.2
  345.3 6.8 %collective-permute-done = bf16[128,2,128]{2,0,1:T(8,128)(2,1)S(1)} collective-permute-done((bf16[128,2,128]{2,0,1:T(8,128)(2,1)S(1)}, bf16[128,2,128]{2,0,1:T(8,128)(2,1)S(1)}, u32[]{:S(2)}, u32[]{:S(2)}) %collective-permute-start) | collective-permute-done | bytes 65568 | tf_op jit(solution)/shard_map/while/body/eval_jaxpr/ppermute | solution.py:12
  352.3 1.7 collective-permute-done.2
  356.4 6.8 %collective-permute-done = bf16[128,2,128]{2,0,1:T(8,128)(2,1)S(1)} collective-permute-done((bf16[128,2,128]{2,0,1:T(8,128)(2,1)S(1)}, bf16[128,2,128]{2,0,1:T(8,128)(2,1)S(1)}, u32[]{:S(2)}, u32[]{:S(2)}) %collective-permute-start) | collective-permute-done | bytes 65568 | tf_op jit(solution)/shard_map/while/body/eval_jaxpr/ppermute | solution.py:12
  363.3 1.7 collective-permute-done.2
  367.5 6.8 %collective-permute-done = bf16[128,2,128]{2,0,1:T(8,128)(2,1)S(1)} collective-permute-done((bf16[128,2,128]{2,0,1:T(8,128)(2,1)S(1)}, bf16[128,2,128]{2,0,1:T(8,128)(2,1)S(1)}, u32[]{:S(2)}, u32[]{:S(2)}) %collective-permute-start) | collective-permute-done | bytes 65568 | tf_op jit(solution)/shard_map/while/body/eval_jaxpr/ppermute | solution.py:12
  374.4 1.7 collective-permute-done.2
  378.6 6.8 %collective-permute-done = bf16[128,2,128]{2,0,1:T(8,128)(2,1)S(1)} collective-permute-done((bf16[128,2,128]{2,0,1:T(8,128)(2,1)S(1)}, bf16[128,2,128]{2,0,1:T(8,128)(2,1)S(1)}, u32[]{:S(2)}, u32[]{:S(2)}) %collective-permute-start) | collective-permute-done | bytes 65568 | tf_op jit(solution)/shard_map/while/body/eval_jaxpr/ppermute | solution.py:12
  385.5 1.7 collective-permute-done.2
  389.7 6.8 %collective-permute-done = bf16[128,2,128]{2,0,1:T(8,128)(2,1)S(1)} collective-permute-done((bf16[128,2,128]{2,0,1:T(8,128)(2,1)S(1)}, bf16[128,2,128]{2,0,1:T(8,128)(2,1)S(1)}, u32[]{:S(2)}, u32[]{:S(2)}) %collective-permute-start) | collective-permute-done | bytes 65568 | tf_op jit(solution)/shard_map/while/body/eval_jaxpr/ppermute | solution.py:12
  396.6 1.7 collective-permute-done.2
  400.7 6.8 %collective-permute-done = bf16[128,2,128]{2,0,1:T(8,128)(2,1)S(1)} collective-permute-done((bf16[128,2,128]{2,0,1:T(8,128)(2,1)S(1)}, bf16[128,2,128]{2,0,1:T(8,128)(2,1)S(1)}, u32[]{:S(2)}, u32[]{:S(2)}) %collective-permute-start) | collective-permute-done | bytes 65568 | tf_op jit(solution)/shard_map/while/body/eval_jaxpr/ppermute | solution.py:12
  407.7 1.7 collective-permute-done.2
  411.8 6.8 %collective-permute-done = bf16[128,2,128]{2,0,1:T(8,128)(2,1)S(1)} collective-permute-done((bf16[128,2,128]{2,0,1:T(8,128)(2,1)S(1)}, bf16[128,2,128]{2,0,1:T(8,128)(2,1)S(1)}, u32[]{:S(2)}, u32[]{:S(2)}) %collective-permute-start) | collective-permute-done | bytes 65568 | tf_op jit(solution)/shard_map/while/body/eval_jaxpr/ppermute | solution.py:12
  422.9 6.8 %collective-permute-done = bf16[128,2,128]{2,0,1:T(8,128)(2,1)S(1)} collective-permute-done((bf16[128,2,128]{2,0,1:T(8,128)(2,1)S(1)}, bf16[128,2,128]{2,0,1:T(8,128)(2,1)S(1)}, u32[]{:S(2)}, u32[]{:S(2)}) %collective-permute-start) | collective-permute-done | bytes 65568 | tf_op jit(solution)/shard_map/while/body/eval_jaxpr/ppermute | solution.py:12
  434.0 6.8 %collective-permute-done = bf16[128,2,128]{2,0,1:T(8,128)(2,1)S(1)} collective-permute-done((bf16[128,2,128]{2,0,1:T(8,128)(2,1)S(1)}, bf16[128,2,128]{2,0,1:T(8,128)(2,1)S(1)}, u32[]{:S(2)}, u32[]{:S(2)}) %collective-permute-start) | collective-permute-done | bytes 65568 | tf_op jit(solution)/shard_map/while/body/eval_jaxpr/ppermute | solution.py:12
  440.9 1.7 collective-permute-done.2
  445.1 6.8 %collective-permute-done = bf16[128,2,128]{2,0,1:T(8,128)(2,1)S(1)} collective-permute-done((bf16[128,2,128]{2,0,1:T(8,128)(2,1)S(1)}, bf16[128,2,128]{2,0,1:T(8,128)(2,1)S(1)}, u32[]{:S(2)}, u32[]{:S(2)}) %collective-permute-start) | collective-permute-done | bytes 65568 | tf_op jit(solution)/shard_map/while/body/eval_jaxpr/ppermute | solution.py:12
  456.2 6.8 %collective-permute-done = bf16[128,2,128]{2,0,1:T(8,128)(2,1)S(1)} collective-permute-done((bf16[128,2,128]{2,0,1:T(8,128)(2,1)S(1)}, bf16[128,2,128]{2,0,1:T(8,128)(2,1)S(1)}, u32[]{:S(2)}, u32[]{:S(2)}) %collective-permute-start) | collective-permute-done | bytes 65568 | tf_op jit(solution)/shard_map/while/body/eval_jaxpr/ppermute | solution.py:12
  467.2 6.8 %collective-permute-done = bf16[128,2,128]{2,0,1:T(8,128)(2,1)S(1)} collective-permute-done((bf16[128,2,128]{2,0,1:T(8,128)(2,1)S(1)}, bf16[128,2,128]{2,0,1:T(8,128)(2,1)S(1)}, u32[]{:S(2)}, u32[]{:S(2)}) %collective-permute-start) | collective-permute-done | bytes 65568 | tf_op jit(solution)/shard_map/while/body/eval_jaxpr/ppermute | solution.py:12
  478.2 7.5 %collective-permute-done.5 = bf16[128,2,128]{0,2,1:T(8,128)(2,1)S(1)} collective-permute-done((bf16[128,2,128]{0,2,1:T(8,128)(2,1)S(1)}, bf16[128,2,128]{0,2,1:T(8,128)(2,1)S(1)}, u32[]{:S(2)}, u32[]{:S(2)}) %collective-permute-start.5) | collective-permute-done | bytes 65568 | tf_op jit(solution)/shard_map/ppermute | solution.py:12
  (509 shorter events, 105.8 us)
Async XLA Ops:
  7.2 42.9 %all-gather.5.cloned.1.call-start = ((), (), s32[]{:S(2)}) async-start(), calls=%async_computation.1 | async-start | bytes 1179648 | tf_op jit(solution)/shard_map/all_gather | solution.py:135
  7.9 127.2 %all-gather.3.cloned.1.call-start = ((), (), s32[]{:S(2)}) async-start(), calls=%async_computation | async-start | bytes 2162688 | tf_op jit(solution)/shard_map/all_gather | solution.py:154
  176.9 9.1 %collective-permute-start.1 = (bf16[128,2,128]{2,0,1:T(8,128)(2,1)S(1)}, bf16[128,2,128]{2,0,1:T(8,128)(2,1)S(1)}, u32[]{:S(2)}, u32[]{:S(2)}) collective-permute-start(bf16[128,2,128]{2,0,1:T(8,128)(2,1)S(1)} %copy.102), channel_id=1, source_target_pairs={{248,0},{0,8},{8,16},{16,24},{24,32},{32,40},{40,48},{48,56},{56,6... | collective-permute-start | bytes 196616 | tf_op jit(solution)/shard_map/while/body/eval_jaxpr/ppermute | solution.py:12
  178.5 9.2 %collective-permute-start.2 = (f32[128,2,128]{2,0,1:T(8,128)S(1)}, f32[128,2,128]{2,0,1:T(8,128)S(1)}, u32[]{:S(2)}, u32[]{:S(2)}) collective-permute-start(f32[128,2,128]{2,0,1:T(8,128)S(1)} %fusion.75), channel_id=1, source_target_pairs={{248,0},{0,8},{8,16},{16,24},{24,32},{32,40},{40,48},{48,56},{56,6... | collective-permute-start | bytes 393224 | tf_op jit(solution)/shard_map/while/body/eval_jaxpr/ppermute | solution.py:12
  189.6 9.2 %collective-permute-start.2 = (f32[128,2,128]{2,0,1:T(8,128)S(1)}, f32[128,2,128]{2,0,1:T(8,128)S(1)}, u32[]{:S(2)}, u32[]{:S(2)}) collective-permute-start(f32[128,2,128]{2,0,1:T(8,128)S(1)} %fusion.75), channel_id=1, source_target_pairs={{248,0},{0,8},{8,16},{16,24},{24,32},{32,40},{40,48},{48,56},{56,6... | collective-permute-start | bytes 393224 | tf_op jit(solution)/shard_map/while/body/eval_jaxpr/ppermute | solution.py:12
  189.9 9.2 %collective-permute-start.3 = (f32[128,2,128]{2,0,1:T(8,128)S(1)}, f32[128,2,128]{2,0,1:T(8,128)S(1)}, u32[]{:S(2)}, u32[]{:S(2)}) collective-permute-start(f32[128,2,128]{2,0,1:T(8,128)S(1)} %fusion.76), channel_id=1, source_target_pairs={{248,0},{0,8},{8,16},{16,24},{24,32},{32,40},{40,48},{48,56},{56,6... | collective-permute-start | bytes 393224 | tf_op jit(solution)/shard_map/while/body/eval_jaxpr/ppermute | solution.py:12
  199.1 9.1 %collective-permute-start.1 = (bf16[128,2,128]{2,0,1:T(8,128)(2,1)S(1)}, bf16[128,2,128]{2,0,1:T(8,128)(2,1)S(1)}, u32[]{:S(2)}, u32[]{:S(2)}) collective-permute-start(bf16[128,2,128]{2,0,1:T(8,128)(2,1)S(1)} %copy.102), channel_id=1, source_target_pairs={{248,0},{0,8},{8,16},{16,24},{24,32},{32,40},{40,48},{48,56},{56,6... | collective-permute-start | bytes 196616 | tf_op jit(solution)/shard_map/while/body/eval_jaxpr/ppermute | solution.py:12
  200.7 9.2 %collective-permute-start.2 = (f32[128,2,128]{2,0,1:T(8,128)S(1)}, f32[128,2,128]{2,0,1:T(8,128)S(1)}, u32[]{:S(2)}, u32[]{:S(2)}) collective-permute-start(f32[128,2,128]{2,0,1:T(8,128)S(1)} %fusion.75), channel_id=1, source_target_pairs={{248,0},{0,8},{8,16},{16,24},{24,32},{32,40},{40,48},{48,56},{56,6... | collective-permute-start | bytes 393224 | tf_op jit(solution)/shard_map/while/body/eval_jaxpr/ppermute | solution.py:12
  201.0 9.2 %collective-permute-start.3 = (f32[128,2,128]{2,0,1:T(8,128)S(1)}, f32[128,2,128]{2,0,1:T(8,128)S(1)}, u32[]{:S(2)}, u32[]{:S(2)}) collective-permute-start(f32[128,2,128]{2,0,1:T(8,128)S(1)} %fusion.76), channel_id=1, source_target_pairs={{248,0},{0,8},{8,16},{16,24},{24,32},{32,40},{40,48},{48,56},{56,6... | collective-permute-start | bytes 393224 | tf_op jit(solution)/shard_map/while/body/eval_jaxpr/ppermute | solution.py:12
  211.8 9.2 %collective-permute-start.2 = (f32[128,2,128]{2,0,1:T(8,128)S(1)}, f32[128,2,128]{2,0,1:T(8,128)S(1)}, u32[]{:S(2)}, u32[]{:S(2)}) collective-permute-start(f32[128,2,128]{2,0,1:T(8,128)S(1)} %fusion.75), channel_id=1, source_target_pairs={{248,0},{0,8},{8,16},{16,24},{24,32},{32,40},{40,48},{48,56},{56,6... | collective-permute-start | bytes 393224 | tf_op jit(solution)/shard_map/while/body/eval_jaxpr/ppermute | solution.py:12
  212.1 9.2 %collective-permute-start.3 = (f32[128,2,128]{2,0,1:T(8,128)S(1)}, f32[128,2,128]{2,0,1:T(8,128)S(1)}, u32[]{:S(2)}, u32[]{:S(2)}) collective-permute-start(f32[128,2,128]{2,0,1:T(8,128)S(1)} %fusion.76), channel_id=1, source_target_pairs={{248,0},{0,8},{8,16},{16,24},{24,32},{32,40},{40,48},{48,56},{56,6... | collective-permute-start | bytes 393224 | tf_op jit(solution)/shard_map/while/body/eval_jaxpr/ppermute | solution.py:12
  222.8 9.2 %collective-permute-start.2 = (f32[128,2,128]{2,0,1:T(8,128)S(1)}, f32[128,2,128]{2,0,1:T(8,128)S(1)}, u32[]{:S(2)}, u32[]{:S(2)}) collective-permute-start(f32[128,2,128]{2,0,1:T(8,128)S(1)} %fusion.75), channel_id=1, source_target_pairs={{248,0},{0,8},{8,16},{16,24},{24,32},{32,40},{40,48},{48,56},{56,6... | collective-permute-start | bytes 393224 | tf_op jit(solution)/shard_map/while/body/eval_jaxpr/ppermute | solution.py:12
  223.2 9.2 %collective-permute-start.3 = (f32[128,2,128]{2,0,1:T(8,128)S(1)}, f32[128,2,128]{2,0,1:T(8,128)S(1)}, u32[]{:S(2)}, u32[]{:S(2)}) collective-permute-start(f32[128,2,128]{2,0,1:T(8,128)S(1)} %fusion.76), channel_id=1, source_target_pairs={{248,0},{0,8},{8,16},{16,24},{24,32},{32,40},{40,48},{48,56},{56,6... | collective-permute-start | bytes 393224 | tf_op jit(solution)/shard_map/while/body/eval_jaxpr/ppermute | solution.py:12
  233.9 9.2 %collective-permute-start.2 = (f32[128,2,128]{2,0,1:T(8,128)S(1)}, f32[128,2,128]{2,0,1:T(8,128)S(1)}, u32[]{:S(2)}, u32[]{:S(2)}) collective-permute-start(f32[128,2,128]{2,0,1:T(8,128)S(1)} %fusion.75), channel_id=1, source_target_pairs={{248,0},{0,8},{8,16},{16,24},{24,32},{32,40},{40,48},{48,56},{56,6... | collective-permute-start | bytes 393224 | tf_op jit(solution)/shard_map/while/body/eval_jaxpr/ppermute | solution.py:12
  234.2 9.2 %collective-permute-start.3 = (f32[128,2,128]{2,0,1:T(8,128)S(1)}, f32[128,2,128]{2,0,1:T(8,128)S(1)}, u32[]{:S(2)}, u32[]{:S(2)}) collective-permute-start(f32[128,2,128]{2,0,1:T(8,128)S(1)} %fusion.76), channel_id=1, source_target_pairs={{248,0},{0,8},{8,16},{16,24},{24,32},{32,40},{40,48},{48,56},{56,6... | collective-permute-start | bytes 393224 | tf_op jit(solution)/shard_map/while/body/eval_jaxpr/ppermute | solution.py:12
  243.4 9.1 %collective-permute-start.1 = (bf16[128,2,128]{2,0,1:T(8,128)(2,1)S(1)}, bf16[128,2,128]{2,0,1:T(8,128)(2,1)S(1)}, u32[]{:S(2)}, u32[]{:S(2)}) collective-permute-start(bf16[128,2,128]{2,0,1:T(8,128)(2,1)S(1)} %copy.102), channel_id=1, source_target_pairs={{248,0},{0,8},{8,16},{16,24},{24,32},{32,40},{40,48},{48,56},{56,6... | collective-permute-start | bytes 196616 | tf_op jit(solution)/shard_map/while/body/eval_jaxpr/ppermute | solution.py:12
  245.0 9.2 %collective-permute-start.2 = (f32[128,2,128]{2,0,1:T(8,128)S(1)}, f32[128,2,128]{2,0,1:T(8,128)S(1)}, u32[]{:S(2)}, u32[]{:S(2)}) collective-permute-start(f32[128,2,128]{2,0,1:T(8,128)S(1)} %fusion.75), channel_id=1, source_target_pairs={{248,0},{0,8},{8,16},{16,24},{24,32},{32,40},{40,48},{48,56},{56,6... | collective-permute-start | bytes 393224 | tf_op jit(solution)/shard_map/while/body/eval_jaxpr/ppermute | solution.py:12
  245.3 9.2 %collective-permute-start.3 = (f32[128,2,128]{2,0,1:T(8,128)S(1)}, f32[128,2,128]{2,0,1:T(8,128)S(1)}, u32[]{:S(2)}, u32[]{:S(2)}) collective-permute-start(f32[128,2,128]{2,0,1:T(8,128)S(1)} %fusion.76), channel_id=1, source_target_pairs={{248,0},{0,8},{8,16},{16,24},{24,32},{32,40},{40,48},{48,56},{56,6... | collective-permute-start | bytes 393224 | tf_op jit(solution)/shard_map/while/body/eval_jaxpr/ppermute | solution.py:12
  256.1 9.2 %collective-permute-start.2 = (f32[128,2,128]{2,0,1:T(8,128)S(1)}, f32[128,2,128]{2,0,1:T(8,128)S(1)}, u32[]{:S(2)}, u32[]{:S(2)}) collective-permute-start(f32[128,2,128]{2,0,1:T(8,128)S(1)} %fusion.75), channel_id=1, source_target_pairs={{248,0},{0,8},{8,16},{16,24},{24,32},{32,40},{40,48},{48,56},{56,6... | collective-permute-start | bytes 393224 | tf_op jit(solution)/shard_map/while/body/eval_jaxpr/ppermute | solution.py:12
  256.4 9.2 %collective-permute-start.3 = (f32[128,2,128]{2,0,1:T(8,128)S(1)}, f32[128,2,128]{2,0,1:T(8,128)S(1)}, u32[]{:S(2)}, u32[]{:S(2)}) collective-permute-start(f32[128,2,128]{2,0,1:T(8,128)S(1)} %fusion.76), channel_id=1, source_target_pairs={{248,0},{0,8},{8,16},{16,24},{24,32},{32,40},{40,48},{48,56},{56,6... | collective-permute-start | bytes 393224 | tf_op jit(solution)/shard_map/while/body/eval_jaxpr/ppermute | solution.py:12
  267.2 9.2 %collective-permute-start.2 = (f32[128,2,128]{2,0,1:T(8,128)S(1)}, f32[128,2,128]{2,0,1:T(8,128)S(1)}, u32[]{:S(2)}, u32[]{:S(2)}) collective-permute-start(f32[128,2,128]{2,0,1:T(8,128)S(1)} %fusion.75), channel_id=1, source_target_pairs={{248,0},{0,8},{8,16},{16,24},{24,32},{32,40},{40,48},{48,56},{56,6... | collective-permute-start | bytes 393224 | tf_op jit(solution)/shard_map/while/body/eval_jaxpr/ppermute | solution.py:12
  267.5 9.2 %collective-permute-start.3 = (f32[128,2,128]{2,0,1:T(8,128)S(1)}, f32[128,2,128]{2,0,1:T(8,128)S(1)}, u32[]{:S(2)}, u32[]{:S(2)}) collective-permute-start(f32[128,2,128]{2,0,1:T(8,128)S(1)} %fusion.76), channel_id=1, source_target_pairs={{248,0},{0,8},{8,16},{16,24},{24,32},{32,40},{40,48},{48,56},{56,6... | collective-permute-start | bytes 393224 | tf_op jit(solution)/shard_map/while/body/eval_jaxpr/ppermute | solution.py:12
  278.3 9.2 %collective-permute-start.2 = (f32[128,2,128]{2,0,1:T(8,128)S(1)}, f32[128,2,128]{2,0,1:T(8,128)S(1)}, u32[]{:S(2)}, u32[]{:S(2)}) collective-permute-start(f32[128,2,128]{2,0,1:T(8,128)S(1)} %fusion.75), channel_id=1, source_target_pairs={{248,0},{0,8},{8,16},{16,24},{24,32},{32,40},{40,48},{48,56},{56,6... | collective-permute-start | bytes 393224 | tf_op jit(solution)/shard_map/while/body/eval_jaxpr/ppermute | solution.py:12
  278.6 9.2 %collective-permute-start.3 = (f32[128,2,128]{2,0,1:T(8,128)S(1)}, f32[128,2,128]{2,0,1:T(8,128)S(1)}, u32[]{:S(2)}, u32[]{:S(2)}) collective-permute-start(f32[128,2,128]{2,0,1:T(8,128)S(1)} %fusion.76), channel_id=1, source_target_pairs={{248,0},{0,8},{8,16},{16,24},{24,32},{32,40},{40,48},{48,56},{56,6... | collective-permute-start | bytes 393224 | tf_op jit(solution)/shard_map/while/body/eval_jaxpr/ppermute | solution.py:12
  287.8 9.1 %collective-permute-start.1 = (bf16[128,2,128]{2,0,1:T(8,128)(2,1)S(1)}, bf16[128,2,128]{2,0,1:T(8,128)(2,1)S(1)}, u32[]{:S(2)}, u32[]{:S(2)}) collective-permute-start(bf16[128,2,128]{2,0,1:T(8,128)(2,1)S(1)} %copy.102), channel_id=1, source_target_pairs={{248,0},{0,8},{8,16},{16,24},{24,32},{32,40},{40,48},{48,56},{56,6... | collective-permute-start | bytes 196616 | tf_op jit(solution)/shard_map/while/body/eval_jaxpr/ppermute | solution.py:12
  289.3 9.2 %collective-permute-start.2 = (f32[128,2,128]{2,0,1:T(8,128)S(1)}, f32[128,2,128]{2,0,1:T(8,128)S(1)}, u32[]{:S(2)}, u32[]{:S(2)}) collective-permute-start(f32[128,2,128]{2,0,1:T(8,128)S(1)} %fusion.75), channel_id=1, source_target_pairs={{248,0},{0,8},{8,16},{16,24},{24,32},{32,40},{40,48},{48,56},{56,6... | collective-permute-start | bytes 393224 | tf_op jit(solution)/shard_map/while/body/eval_jaxpr/ppermute | solution.py:12
  289.6 9.2 %collective-permute-start.3 = (f32[128,2,128]{2,0,1:T(8,128)S(1)}, f32[128,2,128]{2,0,1:T(8,128)S(1)}, u32[]{:S(2)}, u32[]{:S(2)}) collective-permute-start(f32[128,2,128]{2,0,1:T(8,128)S(1)} %fusion.76), channel_id=1, source_target_pairs={{248,0},{0,8},{8,16},{16,24},{24,32},{32,40},{40,48},{48,56},{56,6... | collective-permute-start | bytes 393224 | tf_op jit(solution)/shard_map/while/body/eval_jaxpr/ppermute | solution.py:12
  300.4 9.2 %collective-permute-start.2 = (f32[128,2,128]{2,0,1:T(8,128)S(1)}, f32[128,2,128]{2,0,1:T(8,128)S(1)}, u32[]{:S(2)}, u32[]{:S(2)}) collective-permute-start(f32[128,2,128]{2,0,1:T(8,128)S(1)} %fusion.75), channel_id=1, source_target_pairs={{248,0},{0,8},{8,16},{16,24},{24,32},{32,40},{40,48},{48,56},{56,6... | collective-permute-start | bytes 393224 | tf_op jit(solution)/shard_map/while/body/eval_jaxpr/ppermute | solution.py:12
  300.7 9.2 %collective-permute-start.3 = (f32[128,2,128]{2,0,1:T(8,128)S(1)}, f32[128,2,128]{2,0,1:T(8,128)S(1)}, u32[]{:S(2)}, u32[]{:S(2)}) collective-permute-start(f32[128,2,128]{2,0,1:T(8,128)S(1)} %fusion.76), channel_id=1, source_target_pairs={{248,0},{0,8},{8,16},{16,24},{24,32},{32,40},{40,48},{48,56},{56,6... | collective-permute-start | bytes 393224 | tf_op jit(solution)/shard_map/while/body/eval_jaxpr/ppermute | solution.py:12
  311.5 9.2 %collective-permute-start.2 = (f32[128,2,128]{2,0,1:T(8,128)S(1)}, f32[128,2,128]{2,0,1:T(8,128)S(1)}, u32[]{:S(2)}, u32[]{:S(2)}) collective-permute-start(f32[128,2,128]{2,0,1:T(8,128)S(1)} %fusion.75), channel_id=1, source_target_pairs={{248,0},{0,8},{8,16},{16,24},{24,32},{32,40},{40,48},{48,56},{56,6... | collective-permute-start | bytes 393224 | tf_op jit(solution)/shard_map/while/body/eval_jaxpr/ppermute | solution.py:12
  311.8 9.2 %collective-permute-start.3 = (f32[128,2,128]{2,0,1:T(8,128)S(1)}, f32[128,2,128]{2,0,1:T(8,128)S(1)}, u32[]{:S(2)}, u32[]{:S(2)}) collective-permute-start(f32[128,2,128]{2,0,1:T(8,128)S(1)} %fusion.76), channel_id=1, source_target_pairs={{248,0},{0,8},{8,16},{16,24},{24,32},{32,40},{40,48},{48,56},{56,6... | collective-permute-start | bytes 393224 | tf_op jit(solution)/shard_map/while/body/eval_jaxpr/ppermute | solution.py:12
  322.6 9.2 %collective-permute-start.2 = (f32[128,2,128]{2,0,1:T(8,128)S(1)}, f32[128,2,128]{2,0,1:T(8,128)S(1)}, u32[]{:S(2)}, u32[]{:S(2)}) collective-permute-start(f32[128,2,128]{2,0,1:T(8,128)S(1)} %fusion.75), channel_id=1, source_target_pairs={{248,0},{0,8},{8,16},{16,24},{24,32},{32,40},{40,48},{48,56},{56,6... | collective-permute-start | bytes 393224 | tf_op jit(solution)/shard_map/while/body/eval_jaxpr/ppermute | solution.py:12
  322.9 9.2 %collective-permute-start.3 = (f32[128,2,128]{2,0,1:T(8,128)S(1)}, f32[128,2,128]{2,0,1:T(8,128)S(1)}, u32[]{:S(2)}, u32[]{:S(2)}) collective-permute-start(f32[128,2,128]{2,0,1:T(8,128)S(1)} %fusion.76), channel_id=1, source_target_pairs={{248,0},{0,8},{8,16},{16,24},{24,32},{32,40},{40,48},{48,56},{56,6... | collective-permute-start | bytes 393224 | tf_op jit(solution)/shard_map/while/body/eval_jaxpr/ppermute | solution.py:12
  332.1 9.1 %collective-permute-start.1 = (bf16[128,2,128]{2,0,1:T(8,128)(2,1)S(1)}, bf16[128,2,128]{2,0,1:T(8,128)(2,1)S(1)}, u32[]{:S(2)}, u32[]{:S(2)}) collective-permute-start(bf16[128,2,128]{2,0,1:T(8,128)(2,1)S(1)} %copy.102), channel_id=1, source_target_pairs={{248,0},{0,8},{8,16},{16,24},{24,32},{32,40},{40,48},{48,56},{56,6... | collective-permute-start | bytes 196616 | tf_op jit(solution)/shard_map/while/body/eval_jaxpr/ppermute | solution.py:12
  333.7 9.2 %collective-permute-start.2 = (f32[128,2,128]{2,0,1:T(8,128)S(1)}, f32[128,2,128]{2,0,1:T(8,128)S(1)}, u32[]{:S(2)}, u32[]{:S(2)}) collective-permute-start(f32[128,2,128]{2,0,1:T(8,128)S(1)} %fusion.75), channel_id=1, source_target_pairs={{248,0},{0,8},{8,16},{16,24},{24,32},{32,40},{40,48},{48,56},{56,6... | collective-permute-start | bytes 393224 | tf_op jit(solution)/shard_map/while/body/eval_jaxpr/ppermute | solution.py:12
  334.0 9.2 %collective-permute-start.3 = (f32[128,2,128]{2,0,1:T(8,128)S(1)}, f32[128,2,128]{2,0,1:T(8,128)S(1)}, u32[]{:S(2)}, u32[]{:S(2)}) collective-permute-start(f32[128,2,128]{2,0,1:T(8,128)S(1)} %fusion.76), channel_id=1, source_target_pairs={{248,0},{0,8},{8,16},{16,24},{24,32},{32,40},{40,48},{48,56},{56,6... | collective-permute-start | bytes 393224 | tf_op jit(solution)/shard_map/while/body/eval_jaxpr/ppermute | solution.py:12
  344.7 9.2 %collective-permute-start.2 = (f32[128,2,128]{2,0,1:T(8,128)S(1)}, f32[128,2,128]{2,0,1:T(8,128)S(1)}, u32[]{:S(2)}, u32[]{:S(2)}) collective-permute-start(f32[128,2,128]{2,0,1:T(8,128)S(1)} %fusion.75), channel_id=1, source_target_pairs={{248,0},{0,8},{8,16},{16,24},{24,32},{32,40},{40,48},{48,56},{56,6... | collective-permute-start | bytes 393224 | tf_op jit(solution)/shard_map/while/body/eval_jaxpr/ppermute | solution.py:12
  345.1 9.2 %collective-permute-start.3 = (f32[128,2,128]{2,0,1:T(8,128)S(1)}, f32[128,2,128]{2,0,1:T(8,128)S(1)}, u32[]{:S(2)}, u32[]{:S(2)}) collective-permute-start(f32[128,2,128]{2,0,1:T(8,128)S(1)} %fusion.76), channel_id=1, source_target_pairs={{248,0},{0,8},{8,16},{16,24},{24,32},{32,40},{40,48},{48,56},{56,6... | collective-permute-start | bytes 393224 | tf_op jit(solution)/shard_map/while/body/eval_jaxpr/ppermute | solution.py:12
  355.8 9.2 %collective-permute-start.2 = (f32[128,2,128]{2,0,1:T(8,128)S(1)}, f32[128,2,128]{2,0,1:T(8,128)S(1)}, u32[]{:S(2)}, u32[]{:S(2)}) collective-permute-start(f32[128,2,128]{2,0,1:T(8,128)S(1)} %fusion.75), channel_id=1, source_target_pairs={{248,0},{0,8},{8,16},{16,24},{24,32},{32,40},{40,48},{48,56},{56,6... | collective-permute-start | bytes 393224 | tf_op jit(solution)/shard_map/while/body/eval_jaxpr/ppermute | solution.py:12
  356.1 9.2 %collective-permute-start.3 = (f32[128,2,128]{2,0,1:T(8,128)S(1)}, f32[128,2,128]{2,0,1:T(8,128)S(1)}, u32[]{:S(2)}, u32[]{:S(2)}) collective-permute-start(f32[128,2,128]{2,0,1:T(8,128)S(1)} %fusion.76), channel_id=1, source_target_pairs={{248,0},{0,8},{8,16},{16,24},{24,32},{32,40},{40,48},{48,56},{56,6... | collective-permute-start | bytes 393224 | tf_op jit(solution)/shard_map/while/body/eval_jaxpr/ppermute | solution.py:12
  365.3 9.1 %collective-permute-start.1 = (bf16[128,2,128]{2,0,1:T(8,128)(2,1)S(1)}, bf16[128,2,128]{2,0,1:T(8,128)(2,1)S(1)}, u32[]{:S(2)}, u32[]{:S(2)}) collective-permute-start(bf16[128,2,128]{2,0,1:T(8,128)(2,1)S(1)} %copy.102), channel_id=1, source_target_pairs={{248,0},{0,8},{8,16},{16,24},{24,32},{32,40},{40,48},{48,56},{56,6... | collective-permute-start | bytes 196616 | tf_op jit(solution)/shard_map/while/body/eval_jaxpr/ppermute | solution.py:12
  366.9 9.2 %collective-permute-start.2 = (f32[128,2,128]{2,0,1:T(8,128)S(1)}, f32[128,2,128]{2,0,1:T(8,128)S(1)}, u32[]{:S(2)}, u32[]{:S(2)}) collective-permute-start(f32[128,2,128]{2,0,1:T(8,128)S(1)} %fusion.75), channel_id=1, source_target_pairs={{248,0},{0,8},{8,16},{16,24},{24,32},{32,40},{40,48},{48,56},{56,6... | collective-permute-start | bytes 393224 | tf_op jit(solution)/shard_map/while/body/eval_jaxpr/ppermute | solution.py:12
  367.2 9.2 %collective-permute-start.3 = (f32[128,2,128]{2,0,1:T(8,128)S(1)}, f32[128,2,128]{2,0,1:T(8,128)S(1)}, u32[]{:S(2)}, u32[]{:S(2)}) collective-permute-start(f32[128,2,128]{2,0,1:T(8,128)S(1)} %fusion.76), channel_id=1, source_target_pairs={{248,0},{0,8},{8,16},{16,24},{24,32},{32,40},{40,48},{48,56},{56,6... | collective-permute-start | bytes 393224 | tf_op jit(solution)/shard_map/while/body/eval_jaxpr/ppermute | solution.py:12
  378.0 9.2 %collective-permute-start.2 = (f32[128,2,128]{2,0,1:T(8,128)S(1)}, f32[128,2,128]{2,0,1:T(8,128)S(1)}, u32[]{:S(2)}, u32[]{:S(2)}) collective-permute-start(f32[128,2,128]{2,0,1:T(8,128)S(1)} %fusion.75), channel_id=1, source_target_pairs={{248,0},{0,8},{8,16},{16,24},{24,32},{32,40},{40,48},{48,56},{56,6... | collective-permute-start | bytes 393224 | tf_op jit(solution)/shard_map/while/body/eval_jaxpr/ppermute | solution.py:12
  378.3 9.2 %collective-permute-start.3 = (f32[128,2,128]{2,0,1:T(8,128)S(1)}, f32[128,2,128]{2,0,1:T(8,128)S(1)}, u32[]{:S(2)}, u32[]{:S(2)}) collective-permute-start(f32[128,2,128]{2,0,1:T(8,128)S(1)} %fusion.76), channel_id=1, source_target_pairs={{248,0},{0,8},{8,16},{16,24},{24,32},{32,40},{40,48},{48,56},{56,6... | collective-permute-start | bytes 393224 | tf_op jit(solution)/shard_map/while/body/eval_jaxpr/ppermute | solution.py:12
  389.1 9.2 %collective-permute-start.2 = (f32[128,2,128]{2,0,1:T(8,128)S(1)}, f32[128,2,128]{2,0,1:T(8,128)S(1)}, u32[]{:S(2)}, u32[]{:S(2)}) collective-permute-start(f32[128,2,128]{2,0,1:T(8,128)S(1)} %fusion.75), channel_id=1, source_target_pairs={{248,0},{0,8},{8,16},{16,24},{24,32},{32,40},{40,48},{48,56},{56,6... | collective-permute-start | bytes 393224 | tf_op jit(solution)/shard_map/while/body/eval_jaxpr/ppermute | solution.py:12
  389.4 9.2 %collective-permute-start.3 = (f32[128,2,128]{2,0,1:T(8,128)S(1)}, f32[128,2,128]{2,0,1:T(8,128)S(1)}, u32[]{:S(2)}, u32[]{:S(2)}) collective-permute-start(f32[128,2,128]{2,0,1:T(8,128)S(1)} %fusion.76), channel_id=1, source_target_pairs={{248,0},{0,8},{8,16},{16,24},{24,32},{32,40},{40,48},{48,56},{56,6... | collective-permute-start | bytes 393224 | tf_op jit(solution)/shard_map/while/body/eval_jaxpr/ppermute | solution.py:12
  400.2 9.2 %collective-permute-start.2 = (f32[128,2,128]{2,0,1:T(8,128)S(1)}, f32[128,2,128]{2,0,1:T(8,128)S(1)}, u32[]{:S(2)}, u32[]{:S(2)}) collective-permute-start(f32[128,2,128]{2,0,1:T(8,128)S(1)} %fusion.75), channel_id=1, source_target_pairs={{248,0},{0,8},{8,16},{16,24},{24,32},{32,40},{40,48},{48,56},{56,6... | collective-permute-start | bytes 393224 | tf_op jit(solution)/shard_map/while/body/eval_jaxpr/ppermute | solution.py:12
  400.5 9.2 %collective-permute-start.3 = (f32[128,2,128]{2,0,1:T(8,128)S(1)}, f32[128,2,128]{2,0,1:T(8,128)S(1)}, u32[]{:S(2)}, u32[]{:S(2)}) collective-permute-start(f32[128,2,128]{2,0,1:T(8,128)S(1)} %fusion.76), channel_id=1, source_target_pairs={{248,0},{0,8},{8,16},{16,24},{24,32},{32,40},{40,48},{48,56},{56,6... | collective-permute-start | bytes 393224 | tf_op jit(solution)/shard_map/while/body/eval_jaxpr/ppermute | solution.py:12
  409.7 9.1 %collective-permute-start.1 = (bf16[128,2,128]{2,0,1:T(8,128)(2,1)S(1)}, bf16[128,2,128]{2,0,1:T(8,128)(2,1)S(1)}, u32[]{:S(2)}, u32[]{:S(2)}) collective-permute-start(bf16[128,2,128]{2,0,1:T(8,128)(2,1)S(1)} %copy.102), channel_id=1, source_target_pairs={{248,0},{0,8},{8,16},{16,24},{24,32},{32,40},{40,48},{48,56},{56,6... | collective-permute-start | bytes 196616 | tf_op jit(solution)/shard_map/while/body/eval_jaxpr/ppermute | solution.py:12
  411.2 9.2 %collective-permute-start.2 = (f32[128,2,128]{2,0,1:T(8,128)S(1)}, f32[128,2,128]{2,0,1:T(8,128)S(1)}, u32[]{:S(2)}, u32[]{:S(2)}) collective-permute-start(f32[128,2,128]{2,0,1:T(8,128)S(1)} %fusion.75), channel_id=1, source_target_pairs={{248,0},{0,8},{8,16},{16,24},{24,32},{32,40},{40,48},{48,56},{56,6... | collective-permute-start | bytes 393224 | tf_op jit(solution)/shard_map/while/body/eval_jaxpr/ppermute | solution.py:12
  411.5 9.2 %collective-permute-start.3 = (f32[128,2,128]{2,0,1:T(8,128)S(1)}, f32[128,2,128]{2,0,1:T(8,128)S(1)}, u32[]{:S(2)}, u32[]{:S(2)}) collective-permute-start(f32[128,2,128]{2,0,1:T(8,128)S(1)} %fusion.76), channel_id=1, source_target_pairs={{248,0},{0,8},{8,16},{16,24},{24,32},{32,40},{40,48},{48,56},{56,6... | collective-permute-start | bytes 393224 | tf_op jit(solution)/shard_map/while/body/eval_jaxpr/ppermute | solution.py:12
  422.3 9.2 %collective-permute-start.2 = (f32[128,2,128]{2,0,1:T(8,128)S(1)}, f32[128,2,128]{2,0,1:T(8,128)S(1)}, u32[]{:S(2)}, u32[]{:S(2)}) collective-permute-start(f32[128,2,128]{2,0,1:T(8,128)S(1)} %fusion.75), channel_id=1, source_target_pairs={{248,0},{0,8},{8,16},{16,24},{24,32},{32,40},{40,48},{48,56},{56,6... | collective-permute-start | bytes 393224 | tf_op jit(solution)/shard_map/while/body/eval_jaxpr/ppermute | solution.py:12
  422.6 9.2 %collective-permute-start.3 = (f32[128,2,128]{2,0,1:T(8,128)S(1)}, f32[128,2,128]{2,0,1:T(8,128)S(1)}, u32[]{:S(2)}, u32[]{:S(2)}) collective-permute-start(f32[128,2,128]{2,0,1:T(8,128)S(1)} %fusion.76), channel_id=1, source_target_pairs={{248,0},{0,8},{8,16},{16,24},{24,32},{32,40},{40,48},{48,56},{56,6... | collective-permute-start | bytes 393224 | tf_op jit(solution)/shard_map/while/body/eval_jaxpr/ppermute | solution.py:12
  433.4 9.2 %collective-permute-start.2 = (f32[128,2,128]{2,0,1:T(8,128)S(1)}, f32[128,2,128]{2,0,1:T(8,128)S(1)}, u32[]{:S(2)}, u32[]{:S(2)}) collective-permute-start(f32[128,2,128]{2,0,1:T(8,128)S(1)} %fusion.75), channel_id=1, source_target_pairs={{248,0},{0,8},{8,16},{16,24},{24,32},{32,40},{40,48},{48,56},{56,6... | collective-permute-start | bytes 393224 | tf_op jit(solution)/shard_map/while/body/eval_jaxpr/ppermute | solution.py:12
  433.7 9.2 %collective-permute-start.3 = (f32[128,2,128]{2,0,1:T(8,128)S(1)}, f32[128,2,128]{2,0,1:T(8,128)S(1)}, u32[]{:S(2)}, u32[]{:S(2)}) collective-permute-start(f32[128,2,128]{2,0,1:T(8,128)S(1)} %fusion.76), channel_id=1, source_target_pairs={{248,0},{0,8},{8,16},{16,24},{24,32},{32,40},{40,48},{48,56},{56,6... | collective-permute-start | bytes 393224 | tf_op jit(solution)/shard_map/while/body/eval_jaxpr/ppermute | solution.py:12
  444.5 9.2 %collective-permute-start.2 = (f32[128,2,128]{2,0,1:T(8,128)S(1)}, f32[128,2,128]{2,0,1:T(8,128)S(1)}, u32[]{:S(2)}, u32[]{:S(2)}) collective-permute-start(f32[128,2,128]{2,0,1:T(8,128)S(1)} %fusion.75), channel_id=1, source_target_pairs={{248,0},{0,8},{8,16},{16,24},{24,32},{32,40},{40,48},{48,56},{56,6... | collective-permute-start | bytes 393224 | tf_op jit(solution)/shard_map/while/body/eval_jaxpr/ppermute | solution.py:12
  444.8 9.2 %collective-permute-start.3 = (f32[128,2,128]{2,0,1:T(8,128)S(1)}, f32[128,2,128]{2,0,1:T(8,128)S(1)}, u32[]{:S(2)}, u32[]{:S(2)}) collective-permute-start(f32[128,2,128]{2,0,1:T(8,128)S(1)} %fusion.76), channel_id=1, source_target_pairs={{248,0},{0,8},{8,16},{16,24},{24,32},{32,40},{40,48},{48,56},{56,6... | collective-permute-start | bytes 393224 | tf_op jit(solution)/shard_map/while/body/eval_jaxpr/ppermute | solution.py:12
  454.0 9.1 %collective-permute-start.1 = (bf16[128,2,128]{2,0,1:T(8,128)(2,1)S(1)}, bf16[128,2,128]{2,0,1:T(8,128)(2,1)S(1)}, u32[]{:S(2)}, u32[]{:S(2)}) collective-permute-start(bf16[128,2,128]{2,0,1:T(8,128)(2,1)S(1)} %copy.102), channel_id=1, source_target_pairs={{248,0},{0,8},{8,16},{16,24},{24,32},{32,40},{40,48},{48,56},{56,6... | collective-permute-start | bytes 196616 | tf_op jit(solution)/shard_map/while/body/eval_jaxpr/ppermute | solution.py:12
  455.6 9.2 %collective-permute-start.2 = (f32[128,2,128]{2,0,1:T(8,128)S(1)}, f32[128,2,128]{2,0,1:T(8,128)S(1)}, u32[]{:S(2)}, u32[]{:S(2)}) collective-permute-start(f32[128,2,128]{2,0,1:T(8,128)S(1)} %fusion.75), channel_id=1, source_target_pairs={{248,0},{0,8},{8,16},{16,24},{24,32},{32,40},{40,48},{48,56},{56,6... | collective-permute-start | bytes 393224 | tf_op jit(solution)/shard_map/while/body/eval_jaxpr/ppermute | solution.py:12
  455.9 9.2 %collective-permute-start.3 = (f32[128,2,128]{2,0,1:T(8,128)S(1)}, f32[128,2,128]{2,0,1:T(8,128)S(1)}, u32[]{:S(2)}, u32[]{:S(2)}) collective-permute-start(f32[128,2,128]{2,0,1:T(8,128)S(1)} %fusion.76), channel_id=1, source_target_pairs={{248,0},{0,8},{8,16},{16,24},{24,32},{32,40},{40,48},{48,56},{56,6... | collective-permute-start | bytes 393224 | tf_op jit(solution)/shard_map/while/body/eval_jaxpr/ppermute | solution.py:12
  466.6 9.2 %collective-permute-start.2 = (f32[128,2,128]{2,0,1:T(8,128)S(1)}, f32[128,2,128]{2,0,1:T(8,128)S(1)}, u32[]{:S(2)}, u32[]{:S(2)}) collective-permute-start(f32[128,2,128]{2,0,1:T(8,128)S(1)} %fusion.75), channel_id=1, source_target_pairs={{248,0},{0,8},{8,16},{16,24},{24,32},{32,40},{40,48},{48,56},{56,6... | collective-permute-start | bytes 393224 | tf_op jit(solution)/shard_map/while/body/eval_jaxpr/ppermute | solution.py:12
  467.0 9.2 %collective-permute-start.3 = (f32[128,2,128]{2,0,1:T(8,128)S(1)}, f32[128,2,128]{2,0,1:T(8,128)S(1)}, u32[]{:S(2)}, u32[]{:S(2)}) collective-permute-start(f32[128,2,128]{2,0,1:T(8,128)S(1)} %fusion.76), channel_id=1, source_target_pairs={{248,0},{0,8},{8,16},{16,24},{24,32},{32,40},{40,48},{48,56},{56,6... | collective-permute-start | bytes 393224 | tf_op jit(solution)/shard_map/while/body/eval_jaxpr/ppermute | solution.py:12
  477.1 9.4 %collective-permute-start.4 = (bf16[128,2,128]{2,0,1:T(8,128)(2,1)S(1)}, bf16[128,2,128]{2,0,1:T(8,128)(2,1)S(1)}, u32[]{:S(2)}, u32[]{:S(2)}) collective-permute-start(bf16[128,2,128]{2,0,1:T(8,128)(2,1)S(1)} %fusion.12), channel_id=1, source_target_pairs={{248,0},{0,8},{8,16},{16,24},{24,32},{32,40},{40,48},{48,56},{56,6... | collective-permute-start | bytes 196616 | tf_op jit(solution)/shard_map/ppermute | solution.py:12
  (65 other events, 567.9 us)
Sparse Core Ops, SparseCore 0:
  9.8 40.1 all-gather.4
  53.2 81.8 all-gather.2
where the time goes:
time: 501 us; the launch traced here: 494 us
  waiting for transfers between devices  382 us (76%)
  matrix products  36 us (7%)
  local copies, waits for them, and re-layouts  33.1 us (7%)
  starting transfers between devices  20.9 us (4%)
  between operations  14.2 us (3%)
  other arithmetic  5.27 us (1%)
    ppermute x126, waiting for transfers between devices, shifted(): return lax.ppermute(block, axis, route)  264 us
    all_gather x1, waiting for transfers between devices, shards(): lax.all_gather(keys, 'seq', axis=0, tiled=True)  82.7 us
    all_gather x1, waiting for transfers between devices, shards(): lax.all_gather(out_grad, 'head', axis=1, tiled=True)  34.4 us
    dynamic_slice x32, local copies, waits for them, and re-layouts, advance(): lax.dynamic_slice_in_dim(segment_ids, anchor * tok_rows, tok_rows)  24.5 us
    ppermute x126, starting transfers between devices, shifted(): return lax.ppermute(block, axis, route)  20.8 us
  transfers between devices with their start and end apart: 128, of which 125 were waited for; matrix products, arithmetic and copies ran while one was open for 14% of the time, Pallas kernels for 0%

commit v1 on v0

v1 whole, which is shorter than its diff:
```python
import jax
import jax.numpy as jnp
from jax import lax
from jax.experimental import pallas as pl
from jax.experimental.pallas import tpu as pltpu
from jax.sharding import PartitionSpec as P

HD = 128
TOK = 128
EXTRA = 16
ROWS = TOK + EXTRA
SCALE = HD ** -0.5
LOG2E = 1.4426950408889634
MASKED = -1e30
MESH = pl.DeviceIdType.MESH
BF = jnp.bfloat16
F32 = jnp.float32


def dot_nt(a, b):
    return lax.dot_general(a, b, (((1,), (1,)), ((), ())), preferred_element_type=F32)


def dot_nn(a, b):
    return lax.dot_general(a, b, (((1,), (0,)), ((), ())), preferred_element_type=F32)


def across(row):
    return jnp.broadcast_to(row, (128, 128)).T


def down(column):
    return jnp.broadcast_to(column, (128, 128)).T[0:1, :]


def pieces(x, count):
    out = []
    for _ in range(count):
        high = x.astype(BF).astype(F32)
        out.append(high)
        x = x - high
    return out


def stat_tile(rows, first):
    place = lax.broadcasted_iota(jnp.int32, (EXTRA, 128), 0)
    tile = jnp.zeros((EXTRA, 128), F32)
    for k, row in enumerate(rows):
        tile = jnp.where(place == first + k, jnp.broadcast_to(row, (EXTRA, 128)), tile)
    return tile


def kernel(
    q_ref, k_ref, v_ref, o_ref, og_ref, w_ref, seg_ref,
    dq_ref, dk_ref, dv_ref,
    kb, vqb, gb, ogb, sb, ga, ystage, yin, yout, segc, dlt, mb, lb, dqa, dka, dva,
    ky_s, ky_r, vy_s, vy_r, qy_s, qy_r, gy_s, gy_r, out_s, out_r,
    kz_s, kz_r, kc_s, kc_r, vz_s, vz_r, vc_s, vc_r, gz_s, gz_r, gc_s, gc_r, og_s, og_r,
):
    seq = lax.axis_index("seq")
    head = lax.axis_index("head")
    y = seq // 16
    z = (seq // 2) % 8
    c = seq % 2
    ylo = head // 4
    x = head % 4
    partner = (1 - y) * 16 + z * 2 + c
    sibling = y * 16 + z * 2 + (1 - c)
    right = y * 16 + ((z + 1) % 8) * 2 + c
    left = y * 16 + ((z + 7) % 8) * 2 + c
    mine = pl.ds(pl.multiple_of(y * HD, HD), HD)
    other = pl.ds(pl.multiple_of((1 - y) * HD, HD), HD)

    barrier = pltpu.get_barrier_semaphore()
    for peer in (partner, sibling, right, left):
        pl.semaphore_signal(barrier, inc=1, device_id={"seq": peer}, device_id_type=MESH)
    offsets = [(dy, dx) for dy in range(2) for dx in range(4) if dy or dx]
    for dy, dx in offsets:
        peer = ((ylo + dy) % 2) * 4 + (x + dx) % 4
        pl.semaphore_signal(barrier, inc=1, device_id={"head": peer}, device_id_type=MESH)
    pl.semaphore_wait(barrier, 4 + len(offsets))

    def to_seq(src, dst, ssem, rsem, device):
        return pltpu.make_async_remote_copy(
            src_ref=src, dst_ref=dst, send_sem=ssem, recv_sem=rsem,
            device_id={"seq": device}, device_id_type=MESH)

    def order(e):
        odd = e % 2
        return odd * ((e + 1) // 2) + (1 - odd) * ((8 - e // 2) % 8)

    def z_copy(buf, ssem, rsem, slot, u, rightward):
        there = (slot + 2 * rightward + 7) % 8
        device = y * 16 + ((z + 2 * rightward + 7) % 8) * 2 + c
        return to_seq(buf.at[slot, 0, u], buf.at[there, 0, u], ssem.at[rightward, slot, u],
                      rsem.at[there, u], device)

    def z_arrive(buf, ssem, rsem, slot, u):
        to_seq(buf.at[slot, 0, u], buf.at[slot, 0, u], ssem.at[0, slot, u], rsem.at[slot, u], right).wait_recv()

    def c_copy(buf, ssem, rsem, slot):
        return to_seq(buf.at[slot, 0], buf.at[slot, 1], ssem.at[slot], rsem.at[slot], sibling)

    kring = (kb, kz_s, kz_r, kc_s, kc_r)
    vring = (vqb, vz_s, vz_r, vc_s, vc_r)
    gring = (gb, gz_s, gz_r, gc_s, gc_r)

    def first(ring, u):
        buf, zs, zr, _, _ = ring
        z_copy(buf, zs, zr, 0, u, 1).start()
        z_copy(buf, zs, zr, 0, u, 0).start()

    def relay(ring, e):
        buf, zs, zr, cs, cr = ring
        slot = order(e)
        odd = e % 2
        main = 1 - odd
        z_arrive(buf, zs, zr, slot, main)

        @pl.when(e < 7)
        def _():
            z_copy(buf, zs, zr, slot, main, odd).start()

        z_arrive(buf, zs, zr, slot, odd)

        @pl.when(e < 5)
        def _():
            z_copy(buf, zs, zr, slot, odd, odd).start()

        c_copy(buf, cs, cr, slot).start()

    def settle(ring):
        buf, zs, zr, cs, cr = ring
        for u in range(2):
            for slot in range(0, 4 - u):
                z_copy(buf, zs, zr, slot, u, 1).wait_send()
            for k in range(0, 3 + u):
                z_copy(buf, zs, zr, (8 - k) % 8, u, 0).wait_send()

        def one(slot, carry):
            c_copy(buf, cs, cr, slot).wait_send()
            return carry

        lax.fori_loop(0, 8, one, 0)

    ky = to_seq(k_ref.at[:, other], kb.at[0, 0, 1], ky_s, ky_r, partner)
    vy = to_seq(v_ref.at[:, other], vqb.at[0, 0, 1, 0], vy_s, vy_r, partner)
    qy = to_seq(q_ref.at[:, other], vqb.at[0, 0, 1, 1], qy_s, qy_r, partner)
    ky.start()
    vy.start()
    qy.start()
    kb[0, 0, 0] = k_ref[:, mine]
    first(kring, 0)
    vqb[0, 0, 0, 0] = v_ref[:, mine]
    vqb[0, 0, 0, 1] = q_ref[:, mine]

    og_copies = []
    for n, (dy, dx) in enumerate(offsets):
        peer = ((ylo + dy) % 2) * 4 + (x + dx) % 4
        slot = dy * 4 + (4 - dx) % 4
        og_copies.append(pltpu.make_async_remote_copy(
            src_ref=og_ref, dst_ref=ogb.at[slot], send_sem=og_s.at[dy * 4 + dx], recv_sem=og_r.at[slot],
            device_id={"head": peer}, device_id_type=MESH))
    for copy in og_copies:
        copy.start()

    seg_own = seg_ref[pl.ds(seq, 1), :].astype(F32)
    seg_far = seg_ref[pl.ds(partner, 1), :].astype(F32)
    segc[0:128, :] = across(seg_own)
    segc[128:256, :] = across(seg_far)
    mb[...] = jnp.full(mb.shape, MASKED, F32)
    lb[...] = jnp.zeros(lb.shape, F32)
    dqa[...] = jnp.zeros(dqa.shape, F32)
    dka[...] = jnp.zeros(dka.shape, F32)
    dva[...] = jnp.zeros(dva.shape, F32)

    ky.wait_recv()
    first(kring, 1)
    c_copy(kb, kc_s, kc_r, 0).start()
    vy.wait_recv()
    qy.wait_recv()

    def seg_row(slot):
        zz = (z + 8 - slot) % 8
        rows = []
        for cc in range(2):
            for u in range(2):
                plane = y if u == 0 else 1 - y
                core = c if cc == 0 else 1 - c
                rows.append(seg_ref[pl.ds(plane * 16 + zz * 2 + core, 1), :].astype(F32))
        return jnp.concatenate(rows, axis=1)

    def columns(slot):
        return pl.ds(pl.multiple_of(slot * 512, 512), 512)

    def wide(tile):
        return jnp.concatenate([tile] * 4, axis=1)

    def have(ring, slot):
        buf, _, _, cs, cr = ring
        c_copy(buf, cs, cr, slot).wait_recv()

    def pass_a(e):
        slot = order(e)
        keys = kb[slot].reshape(512, HD)
        row = seg_row(slot)
        for half in range(2):
            part = pl.ds(half * 128, 128)
            s = dot_nt(vqb[0, 0, half, 1], keys)
            s = jnp.where(wide(segc[part, :]) == row, s, MASKED)
            sb[part, columns(slot)] = s
            top = jnp.maximum(jnp.maximum(s[:, 0:128], s[:, 128:256]), jnp.maximum(s[:, 256:384], s[:, 384:512]))
            mb[part, :] = jnp.maximum(mb[part, :], top)

    def pass_b(e):
        slot = order(e)
        for half in range(2):
            part = pl.ds(half * 128, 128)
            p = jnp.exp2((sb[part, columns(slot)] - wide(mb[part, :])) * (SCALE * LOG2E))
            sb[part, columns(slot)] = p
            lb[part, :] += (p[:, 0:128] + p[:, 128:256]) + (p[:, 256:384] + p[:, 384:512])

    def pass_c(e):
        slot = order(e)
        vals = vqb[slot, :, :, 0].reshape(512, HD)
        keys = kb[slot].reshape(512, HD)
        for half in range(2):
            part = pl.ds(half * 128, 128)
            dp = dot_nt(gb[0, 0, half, 0:128], vals)
            ds = sb[part, columns(slot)] * (dp - wide(dlt[part, :]))
            dqa[part, :] += dot_nn(ds.astype(BF), keys)

    def pass_k(e):
        slot = order(e)
        quer = vqb[slot, :, :, 1].reshape(512, HD)
        grad = gb[slot, :, :, 0:128].reshape(512, HD)
        row = seg_row(slot)
        deltas, logs = [], []
        for cc in range(2):
            for u in range(2):
                stats = gb[slot, cc, u, 128:144].astype(F32)
                deltas.append(stats[0:1] + stats[1:2])
                logs.append((stats[2:3] + stats[3:4]) + stats[4:5])
        deltas = jnp.concatenate(deltas, axis=1)
        logs = jnp.concatenate(logs, axis=1) * LOG2E
        for half in range(2):
            part = pl.ds(half * 128, 128)
            s = dot_nt(kb[0, 0, half], quer) * (SCALE * LOG2E) - logs
            p = jnp.exp2(jnp.where(wide(segc[part, :]) == row, s, MASKED))
            dva[part, :] += dot_nn(p.astype(BF), grad)
            dp = dot_nt(vqb[0, 0, half, 0], grad)
            ds = p * (dp - deltas)
            dka[part, :] += dot_nn(ds.astype(BF), quer)

    def make_grad():
        acc = None
        for slot in range(8):
            dy, dx = slot // 4, slot % 4
            block = ((ylo + dy) % 2) * 4 + (x + dx) % 4
            if slot:
                pltpu.make_async_remote_copy(
                    src_ref=og_ref, dst_ref=ogb.at[slot], send_sem=og_s.at[slot], recv_sem=og_r.at[slot],
                    device_id={"head": head}, device_id_type=MESH).wait_recv()
                part = ogb[slot]
            else:
                part = og_ref[...]
            term = dot_nt(part, w_ref[:, pl.ds(pl.multiple_of(block * 512, 512), 512)])
            acc = term if acc is None else acc + term
        ga[...] = acc.astype(BF)
        grad_far = ga[:, other]
        grad_own = ga[:, mine]
        far = (grad_far.astype(F32) * o_ref[:, other].astype(F32)).T
        own = grad_own.astype(F32) * o_ref[:, mine].astype(F32)
        far_row = jnp.sum(far, axis=0, keepdims=True)
        own_col = jnp.sum(own, axis=1, keepdims=True)
        ystage[0:128, :] = grad_far
        ystage[128:144, :] = stat_tile(pieces(far_row, 2), 0).astype(BF)
        to_seq(ystage, gb.at[0, 0, 1], gy_s, gy_r, partner).start()
        gb[0, 0, 0, 0:128] = grad_own
        dlt[0:128, :] = jnp.broadcast_to(own_col, (128, 128))

    def ring_step(e, carry):
        @pl.when(e >= 1)
        def _():
            relay(kring, e)

        @pl.when(e == 1)
        def _():
            first(vring, 0)
            first(vring, 1)
            c_copy(vqb, vc_s, vc_r, 0).start()

        @pl.when(e >= 3)
        def _():
            relay(vring, e - 2)

        @pl.when(e >= 1)
        def _():
            have(kring, order(e - 1))
            pass_a(e - 1)

        @pl.when(e == 6)
        def _():
            make_grad()

        return carry

    lax.fori_loop(0, 8, ring_step, 0)
    have(kring, order(7))
    pass_a(7)
    relay(vring, 6)
    top = jnp.max(mb[...], axis=1, keepdims=True)
    mb[...] = jnp.broadcast_to(top, mb.shape)

    def b_step(e, carry):
        pass_b(e)
        return carry

    lax.fori_loop(0, 8, b_step, 0)
    total = jnp.sum(lb[...], axis=1, keepdims=True)
    lb[...] = jnp.broadcast_to(SCALE / total, lb.shape)
    logs = top * SCALE + jnp.log(total)
    gb[0, 0, 0, 128:144] = (
        stat_tile(pieces(down(dlt[0:128, 0:1]), 2), 0)
        + stat_tile(pieces(down(logs[0:128]), 3), 2)
    ).astype(BF)
    first(gring, 0)
    to_seq(ystage, gb.at[0, 0, 1], gy_s, gy_r, partner).wait_recv()
    stats = gb[0, 0, 1, 128:144].astype(F32)
    dlt[128:256, :] = across(stats[0:1] + stats[1:2])
    gb[0, 0, 1, 128:144] = (stats + stat_tile(pieces(down(logs[128:256]), 3), 2)).astype(BF)
    first(gring, 1)
    c_copy(gb, gc_s, gc_r, 0).start()
    relay(vring, 7)

    def last_step(e, carry):
        @pl.when(e < 8)
        def _():
            relay(gring, e)

        have(vring, order(e - 1))
        pass_c(e - 1)
        have(gring, order(e - 1))
        pass_k(e - 1)
        return carry

    lax.fori_loop(1, 9, last_step, 0)

    results = (dqa[...] * lb[...], dka[...] * SCALE, dva[...])
    outs = []
    for n, value in enumerate(results):
        yout[n] = value[128:256].astype(BF)
        copy = to_seq(yout.at[n], yin.at[n], out_s.at[n], out_r.at[n], partner)
        copy.start()
        outs.append(copy)
    for n, (value, ref) in enumerate(zip(results, (dq_ref, dk_ref, dv_ref))):
        ref[:, mine] = value[0:128].astype(BF)
    for n, ref in enumerate((dq_ref, dk_ref, dv_ref)):
        outs[n].wait_recv()
        ref[:, other] = yin[n]

    for copy in (ky, vy, qy, *outs, *og_copies):
        copy.wait_send()
    to_seq(ystage, gb.at[0, 0, 1], gy_s, gy_r, partner).wait_send()
    for ring in (kring, vring, gring):
        settle(ring)


def shards(queries, keys, values, attn_out, out_grad, out_weight, segment_ids):
    vmem = pl.BlockSpec(memory_space=pltpu.VMEM)
    dma = pltpu.SemaphoreType.DMA
    out = jax.ShapeDtypeStruct((TOK, 2 * HD), BF)
    ring_sems = [dma((2, 8, 2)), dma((8, 2)), dma((8,)), dma((8,))]
    return pl.pallas_call(
        kernel,
        out_shape=(out, out, out),
        in_specs=[vmem] * 7,
        out_specs=(vmem, vmem, vmem),
        scratch_shapes=[
            pltpu.VMEM((8, 2, 2, TOK, HD), BF),
            pltpu.VMEM((8, 2, 2, 2, TOK, HD), BF),
            pltpu.VMEM((8, 2, 2, ROWS, HD), BF),
            pltpu.VMEM((8, TOK, 512), BF),
            pltpu.VMEM((256, 4096), F32),
            pltpu.VMEM((TOK, 2 * HD), BF),
            pltpu.VMEM((ROWS, HD), BF),
            pltpu.VMEM((3, TOK, HD), BF),
            pltpu.VMEM((3, TOK, HD), BF),
            pltpu.VMEM((256, HD), F32),
            pltpu.VMEM((256, HD), F32),
            pltpu.VMEM((256, HD), F32),
            pltpu.VMEM((256, HD), F32),
            pltpu.VMEM((256, HD), F32),
            pltpu.VMEM((256, HD), F32),
            pltpu.VMEM((256, HD), F32),
            dma, dma, dma, dma, dma, dma, dma, dma, dma((3,)), dma((3,)),
            *ring_sems, *ring_sems, *ring_sems,
            dma((8,)), dma((8,)),
        ],
        compiler_params=pltpu.CompilerParams(
            collective_id=0, has_side_effects=True, vmem_limit_bytes=40 * 1024 * 1024),
    )(queries, keys, values, attn_out, out_grad, out_weight, segment_ids.reshape(32, 128))


def solution(mesh):
    return jax.shard_map(
        shards,
        mesh=mesh,
        in_specs=(
            P("seq", "head"),
            P("seq", "head"),
            P("seq", "head"),
            P("seq", "head"),
            P("seq", "head"),
            P("head", None),
            P(),
        ),
        out_specs=(P("seq", "head"), P("seq", "head"), P("seq", "head")),
        check_vma=False,
    )
```

time: 501 us -> 66.6 us (0.13); the launches traced: 494 us -> 66.3 us
  waiting for transfers between devices: 382 us -> 0 us
  Pallas kernels: 0 us -> 57.2 us
  matrix products: 36 us -> 0 us
  local copies, waits for them, and re-layouts: 33.1 us -> 8.45 us
  starting transfers between devices: 20.9 us -> 0 us
  between operations: 14.2 us -> 0.66 us
  other arithmetic: 5.27 us -> 0 us
    ppermute x126 -> x0, waiting for transfers between devices: 264 us -> none  [shifted(): return lax.ppermute(block, axis, route)]
    all_gather x2 -> x0, waiting for transfers between devices: 117 us -> none  [the longest x1 82.7 us: shards(): lax.all_gather(keys, 'seq', axis=0, tiled=True)]
    pallas_call x0 -> x1, Pallas kernels: none -> 57.2 us  [shards(): pl.pallas_call(kernel, out_shape=(out, out, out), in_specs=[vmem] * 7, ou...]
    dot_general x162 -> x0, matrix products: 36 us -> none  [the longest x32 7.01 us: tile_grads(): jnp.einsum('hqk,qhd->khd', score_low, query_part, preferred_element_type=...]
    dynamic_slice x32 -> x0, local copies, waits for them, and re-layouts: 24.5 us -> none  [advance(): lax.dynamic_slice_in_dim(segment_ids, anchor * tok_rows, tok_rows)]
    ppermute x126 -> x0, starting transfers between devices: 20.8 us -> none  [shifted(): return lax.ppermute(block, axis, route)]
  transfers between devices with their start and end apart: 128 -> 0, of which waited for: 125 -> 0; matrix products, arithmetic and copies ran while one was open for 14% -> 0% of each run, Pallas kernels for 0% -> 0%
where the time goes in v1:
time: 66.6 us; the launch traced here: 66.3 us
  Pallas kernels  57.2 us (86%)
  local copies, waits for them, and re-layouts  8.45 us (13%)
    pallas_call x1, Pallas kernels, shards(): pl.pallas_call(kernel, out_shape=(out, out, out), in_specs=[vmem] * 7, ou...  57.2 us
    unnamed x17, local copies, waits for them, and re-layouts  8.45 us

profile of v1, /device:TPU:1, one launch (start us, length us, event | category | flops | bytes accessed | tf_op | source)
XLA Modules:
  0.0 66.3 jit_solution(3880473432277500254)
XLA Ops:
  0.6 0.0 copy-start
  0.6 1.6 %copy-done = bf16[256,4096]{1,0:T(8,128)(2,1)S(1)} copy-done((bf16[256,4096]{1,0:T(8,128)(2,1)S(1)}, bf16[256,4096]{1,0:T(8,128)(2,1)}, u32[]{:S(2)}) %copy-start) | copy-done | bytes 2097176
  2.2 0.0 copy-start.1
  2.2 0.9 %copy-done.1 = bf16[128,512]{1,0:T(8,128)(2,1)S(1)} copy-done((bf16[128,512]{1,0:T(8,128)(2,1)S(1)}, bf16[128,512]{1,0:T(8,128)(2,1)}, u32[]{:S(2)}) %copy-start.1) | copy-done | bytes 131096
  3.1 0.0 copy-start.2
  3.1 0.8 %copy-done.2 = bf16[128,256]{1,0:T(8,128)(2,1)S(1)} copy-done((bf16[128,256]{1,0:T(8,128)(2,1)S(1)}, bf16[128,256]{1,0:T(8,128)(2,1)}, u32[]{:S(2)}) %copy-start.2) | copy-done | bytes 65560
  4.0 0.0 copy-start.3
  4.0 0.8 %copy-done.3 = bf16[128,256]{1,0:T(8,128)(2,1)S(1)} copy-done((bf16[128,256]{1,0:T(8,128)(2,1)S(1)}, bf16[128,256]{1,0:T(8,128)(2,1)}, u32[]{:S(2)}) %copy-start.3) | copy-done | bytes 65560
  4.8 0.0 copy-start.4
  4.8 0.8 %copy-done.4 = bf16[128,256]{1,0:T(8,128)(2,1)S(1)} copy-done((bf16[128,256]{1,0:T(8,128)(2,1)S(1)}, bf16[128,256]{1,0:T(8,128)(2,1)}, u32[]{:S(2)}) %copy-start.4) | copy-done | bytes 65560
  5.6 0.0 copy-start.5
  5.7 0.8 %copy-done.5 = bf16[128,256]{1,0:T(8,128)(2,1)S(1)} copy-done((bf16[128,256]{1,0:T(8,128)(2,1)S(1)}, bf16[128,256]{1,0:T(8,128)(2,1)}, u32[]{:S(2)}) %copy-start.5) | copy-done | bytes 65560
  6.5 0.0 copy-start.6
  6.5 0.7 %copy-done.6 = s32[4096]{0:T(1024)S(1)} copy-done((s32[4096]{0:T(1024)S(1)}, s32[4096]{0:T(1024)}, u32[]{:S(2)}) %copy-start.6) | copy-done | bytes 16408
  7.2 57.2 %shard_map.94 = (bf16[128,256]{1,0:T(8,128)(2,1)S(1)}, bf16[128,256]{1,0:T(8,128)(2,1)S(1)}, bf16[128,256]{1,0:T(8,128)(2,1)S(1)}) custom-call(bf16[128,256]{1,0:T(8,128)(2,1)S(1)} %copy-done.2, bf16[128,256]{1,0:T(8,128)(2,1)S(1)} %copy-done.3, bf16[128,256]{1,0:T(8,128)(2,1)S(1)} %copy-done.4, bf16[128,256]{1,0:T(8,128)(2,1)S(1)} %copy-done.5, ...), custom_call_target="tpu_custom_call" | custom-call | tf_op jit(solution)/shard_map/pallas_call | solution.py:374
  64.4 0.6 copy.13
  65.0 0.6 copy.14
  65.6 0.6 copy.15
Async XLA Ops:
  0.6 1.6 %copy-start = (bf16[256,4096]{1,0:T(8,128)(2,1)S(1)}, bf16[256,4096]{1,0:T(8,128)(2,1)}, u32[]{:S(2)}) copy-start(bf16[256,4096]{1,0:T(8,128)(2,1)} %w_ref.1) | copy-start | bytes 6291460
  2.2 0.9 %copy-start.1 = (bf16[128,512]{1,0:T(8,128)(2,1)S(1)}, bf16[128,512]{1,0:T(8,128)(2,1)}, u32[]{:S(2)}) copy-start(bf16[128,512]{1,0:T(8,128)(2,1)} %og_ref.1) | copy-start | bytes 393220
  3.1 0.8 %copy-start.2 = (bf16[128,256]{1,0:T(8,128)(2,1)S(1)}, bf16[128,256]{1,0:T(8,128)(2,1)}, u32[]{:S(2)}) copy-start(bf16[128,256]{1,0:T(8,128)(2,1)} %q_ref.1) | copy-start | bytes 196612
  4.0 0.8 %copy-start.3 = (bf16[128,256]{1,0:T(8,128)(2,1)S(1)}, bf16[128,256]{1,0:T(8,128)(2,1)}, u32[]{:S(2)}) copy-start(bf16[128,256]{1,0:T(8,128)(2,1)} %k_ref.1) | copy-start | bytes 196612
  4.8 0.8 %copy-start.4 = (bf16[128,256]{1,0:T(8,128)(2,1)S(1)}, bf16[128,256]{1,0:T(8,128)(2,1)}, u32[]{:S(2)}) copy-start(bf16[128,256]{1,0:T(8,128)(2,1)} %v_ref.1) | copy-start | bytes 196612
  5.6 0.8 %copy-start.5 = (bf16[128,256]{1,0:T(8,128)(2,1)S(1)}, bf16[128,256]{1,0:T(8,128)(2,1)}, u32[]{:S(2)}) copy-start(bf16[128,256]{1,0:T(8,128)(2,1)} %o_ref.1) | copy-start | bytes 196612
  6.5 0.7 %copy-start.6 = (s32[4096]{0:T(1024)S(1)}, s32[4096]{0:T(1024)}, u32[]{:S(2)}) copy-start(s32[4096]{0:T(1024)} %param.13) | copy-start | bytes 49156

commit v2 on v0

v2 whole, which is shorter than its diff:
```python
import jax
import jax.numpy as jnp
from jax import lax
from jax.experimental import pallas as pl
from jax.experimental.pallas import tpu as pltpu
from jax.sharding import PartitionSpec as P

HD = 128
TOK = 128
EXTRA = 16
ROWS = TOK + EXTRA
SCALE = HD ** -0.5
LOG2E = 1.4426950408889634
MASKED = -1e30
FLOOR = -1e29
MESH = pl.DeviceIdType.MESH
BF = jnp.bfloat16
F32 = jnp.float32

SEQ_PEERS = (
    (0, -1, 0), (0, 1, 0), (0, 2, 0), (0, -2, 0), (0, -3, 0),
    (0, 0, 1), (0, 1, 1), (0, -1, 1), (0, 3, 1), (0, -3, 1), (0, -2, 1),
    (1, 0, 0), (1, 1, 0), (1, 0, 1), (1, 1, 1), (1, -1, 1),
)
HEAD_PEERS = tuple((dy, dx) for dy in range(2) for dx in range(4) if dy or dx)
QUERY_STEPS = ((0, -1, 2, -3), (0, 1, -2, 3))


def dot_nt(a, b):
    return lax.dot_general(a, b, (((1,), (1,)), ((), ())), preferred_element_type=F32)


def dot_nn(a, b):
    return lax.dot_general(a, b, (((1,), (0,)), ((), ())), preferred_element_type=F32)


def across(row):
    return jnp.broadcast_to(row, (128, 128)).T


def pieces(x, count):
    out = []
    for _ in range(count):
        high = x.astype(BF).astype(F32)
        out.append(high)
        x = x - high
    return out


def stat_tile(rows):
    place = lax.broadcasted_iota(jnp.int32, (EXTRA, 128), 0)
    tile = jnp.zeros((EXTRA, 128), F32)
    for k, row in enumerate(rows):
        tile = jnp.where(place == k, jnp.broadcast_to(row, (EXTRA, 128)), tile)
    return tile.astype(BF)


def kernel(
    q_hbm, k_hbm, v_hbm, o_hbm, og_hbm, w_hbm, seg_hbm,
    dq_hbm, dk_hbm, dv_hbm,
    qb, kb, vb, gb, ogb, ls_in, ls_out, w_ref, o_ref, seg_ref, segk, kt, pb, mb, ga, gstage,
    dka, dva, dq_out, dq_own, dq_in, dkv_out, dkv_in, res,
    w_sem, o_sem, seg_sem, og_sem, own_sem, res_sem,
    q_s, q_r, k_s, k_r, v_s, v_r, g_s, g_r, og_s, og_r, ls_s, ls_r, dq_s, dq_r, dkv_s, dkv_r,
):
    seq = lax.axis_index("seq")
    head = lax.axis_index("head")
    y = seq // 16
    z = (seq // 2) % 8
    c = seq % 2
    ylo = head // 4
    x = head % 4
    sgn = 1 - 2 * ((z + c) % 2)

    def cols(other_head):
        h = 1 - c if other_head else c
        return pl.ds(pl.multiple_of(h * HD, HD), HD)

    def device(dy, steps, dc):
        yy = (1 - y) if dy else y
        return yy * 16 + ((z + 8 + sgn * steps) % 8) * 2 + (c + dc) % 2

    def to_seq(src, dst, ssem, rsem, target):
        return pltpu.make_async_remote_copy(
            src_ref=src, dst_ref=dst, send_sem=ssem, recv_sem=rsem,
            device_id={"seq": target}, device_id_type=MESH)

    def to_head(src, dst, ssem, rsem, target):
        return pltpu.make_async_remote_copy(
            src_ref=src, dst_ref=dst, send_sem=ssem, recv_sem=rsem,
            device_id={"head": target}, device_id_type=MESH)

    local = [
        pltpu.make_async_copy(k_hbm.at[:, cols(0)], kb.at[0, 0, 0], own_sem.at[0]),
        pltpu.make_async_copy(q_hbm.at[:, cols(0)], qb.at[0, 0], own_sem.at[1]),
        pltpu.make_async_copy(v_hbm.at[:, cols(0)], vb.at[0, 0, 0], own_sem.at[2]),
        pltpu.make_async_copy(seg_hbm, seg_ref, seg_sem),
        pltpu.make_async_copy(og_hbm, ogb.at[0], og_sem),
        pltpu.make_async_copy(o_hbm, o_ref, o_sem),
        pltpu.make_async_copy(w_hbm, w_ref, w_sem),
    ]
    for copy in local:
        copy.start()

    barrier = pltpu.get_barrier_semaphore()
    for peer in SEQ_PEERS:
        pl.semaphore_signal(barrier, inc=1, device_id={"seq": device(*peer)}, device_id_type=MESH)
    for dy, dx in HEAD_PEERS:
        peer = ((ylo + dy) % 2) * 4 + (x + dx) % 4
        pl.semaphore_signal(barrier, inc=1, device_id={"head": peer}, device_id_type=MESH)
    pl.semaphore_wait(barrier, len(SEQ_PEERS) + len(HEAD_PEERS))

    sent = []

    def go(copy):
        copy.start()
        sent.append(copy)

    def spread_keys(src, buf, ss, rs):
        for cc in range(2):
            for dy in range(2):
                for dz in range(2):
                    if cc or dy or dz:
                        steps = (-dz if cc else dz)
                        go(to_seq(src.at[:, cols(cc)], buf.at[dy, dz, cc], ss.at[dy, dz, cc], rs.at[dy, dz, cc],
                                  device(dy, steps, cc)))

    spread_keys(k_hbm, kb, k_s, k_r)
    for cc in range(2):
        for d in range(4):
            if cc or d:
                go(to_seq(q_hbm.at[:, cols(cc)], qb.at[d, cc], q_s.at[d, cc], q_r.at[d, cc],
                          device(0, QUERY_STEPS[cc][d], cc)))
    for dy, dx in HEAD_PEERS:
        peer = ((ylo + dy) % 2) * 4 + (x + dx) % 4
        slot = dy * 4 + (4 - dx) % 4
        go(to_head(og_hbm, ogb.at[slot], og_s.at[dy * 4 + dx], og_r.at[slot], peer))
    spread_keys(v_hbm, vb, v_s, v_r)

    for copy in local:
        copy.wait()

    for dy in range(2):
        for dz in range(2):
            for cc in range(2):
                row = seg_ref[pl.ds(device(dy, dz, cc), 1), :].astype(F32)
                segk[dy * 4 + dz * 2 + cc] = across(row)

    def query_segments(d):
        rows = [seg_ref[pl.ds(device(0, -d, cc), 1), :].astype(F32) for cc in range(2)]
        return jnp.concatenate(rows, axis=1)

    def arrived(buf, rs, *at):
        to_seq(buf.at[at], buf.at[at], rs.at[at], rs.at[at], seq).wait_recv()

    def keys_arrived(buf, rs):
        for dy in range(2):
            for dz in range(2):
                for cc in range(2):
                    if cc or dy or dz:
                        arrived(buf, rs, dy, dz, cc)

    keys_arrived(kb, k_r)
    for dy in range(2):
        for dz in range(2):
            for cc in range(2):
                n = dy * 4 + dz * 2 + cc
                kt[:, n * 128:(n + 1) * 128] = kb[dy, dz, cc].astype(F32).T.astype(BF)

    def chunk(n):
        return n // 2, n % 2

    def queries_arrived(buf, rs, d):
        @pl.when(d > 0)
        def _():
            arrived(buf, rs, d, 0)

        arrived(buf, rs, d, 1)

    def owner(d, cc):
        return device(0, -d, cc)

    def score_step(d, carry):
        queries_arrived(qb, q_r, d)
        quer = qb[d].reshape(256, HD)
        row = query_segments(d)
        top = jnp.full((8, 256), FLOOR, F32)
        for n in range(4):
            dy, dz = chunk(n)
            s = dot_nt(kb[dy, dz].reshape(256, HD), quer)
            seg = segk[2 * n:2 * n + 2].reshape(256, 128)
            s = jnp.where(jnp.concatenate([seg, seg], axis=1) == row, s, MASKED)
            pb[d, n * 256:(n + 1) * 256] = s
            top = jnp.maximum(top, jnp.max(s.reshape(32, 8, 256), axis=0))
        top = jnp.max(top, axis=0, keepdims=True)
        total = jnp.zeros((8, 256), F32)
        for n in range(4):
            p = jnp.exp2((pb[d, n * 256:(n + 1) * 256] - top) * (SCALE * LOG2E))
            pb[d, n * 256:(n + 1) * 256] = p
            total = total + jnp.sum(p.reshape(32, 8, 256), axis=0)
        total = jnp.sum(total, axis=0, keepdims=True)
        mb[d] = jnp.broadcast_to(top * SCALE, (8, 256))
        logs = jnp.where(total > 0.0, top * SCALE + jnp.log(jnp.maximum(total, 1e-37)), MASKED)
        for cc in range(2):
            ls_out[d, cc] = jnp.broadcast_to(logs[:, cc * 128:(cc + 1) * 128], (8, 128))

        @pl.when(d > 0)
        def _():
            to_seq(ls_out.at[d, 0], ls_in.at[d, 0], ls_s.at[d, 0], ls_r.at[d, 0], owner(d, 0)).start()

        to_seq(ls_out.at[d, 1], ls_in.at[d, 1], ls_s.at[d, 1], ls_r.at[d, 1], owner(d, 1)).start()
        return carry

    lax.fori_loop(0, 4, score_step, 0)

    logs = []
    for cc in range(2):
        parts = []
        for d in range(4):
            if cc or d:
                arrived(ls_in, ls_r, d, cc)
                parts.append(ls_in[d, cc][0:1])
            else:
                parts.append(ls_out[0, 0][0:1])
        top = jnp.maximum(jnp.maximum(parts[0], parts[1]), jnp.maximum(parts[2], parts[3]))
        total = sum(jnp.exp(part - top) for part in parts)
        logs.append(top + jnp.log(total))

    acc = None
    for slot in range(8):
        block = ((ylo + slot // 4) % 2) * 4 + (x + slot) % 4
        if slot:
            to_head(og_hbm, ogb.at[slot], og_s.at[slot], og_r.at[slot], head).wait_recv()
        term = dot_nt(ogb[slot], w_ref[:, pl.ds(pl.multiple_of(block * 512, 512), 512)])
        acc = term if acc is None else acc + term
    ga[...] = acc.astype(BF)
    for cc in range(2):
        grad = ga[:, cols(cc)]
        delta = jnp.sum((grad.astype(F32) * o_ref[:, cols(cc)].astype(F32)).T, axis=0, keepdims=True)
        gstage[cc, 0:128] = grad
        gstage[cc, 128:144] = stat_tile(pieces(delta, 2) + pieces(logs[cc], 3))
    for d in range(4):
        for cc in range(2):
            if cc or d:
                go(to_seq(gstage.at[cc], gb.at[d, cc], g_s.at[d, cc], g_r.at[d, cc],
                          device(0, QUERY_STEPS[cc][d], cc)))
    gb[0, 0] = gstage[0]

    dka[...] = jnp.zeros(dka.shape, F32)
    dva[...] = jnp.zeros(dva.shape, F32)
    keys_arrived(vb, v_r)

    def grad_step(d, carry):
        queries_arrived(gb, g_r, d)
        quer = qb[d].reshape(256, HD)
        grad = gb[d, :, 0:128].reshape(256, HD)
        deltas, logs = [], []
        for cc in range(2):
            stats = gb[d, cc, 128:144].astype(F32)
            deltas.append(stats[0:1] + stats[1:2])
            logs.append((stats[2:3] + stats[3:4]) + stats[4:5])
        deltas = jnp.concatenate(deltas, axis=1)
        share = jnp.exp(mb[d][0:1] - jnp.concatenate(logs, axis=1))
        dqt = jnp.zeros((HD, 256), F32)
        for n in range(4):
            part = pl.ds(n * 256, 256)
            dy, dz = chunk(n)
            p = pb[d, part] * share
            dva[part] += dot_nn(p.astype(BF), grad)
            dp = dot_nt(vb[dy, dz].reshape(256, HD), grad)
            ds = (p * (dp - deltas)).astype(BF)
            dka[part] += dot_nn(ds, quer)
            dqt = dqt + dot_nn(kt[:, n * 256:(n + 1) * 256], ds)
        for cc in range(2):
            dq_out[d, cc] = dqt[:, cc * 128:(cc + 1) * 128].T.astype(BF)

        @pl.when(d > 0)
        def _():
            to_seq(dq_out.at[d, 0], dq_in.at[d, 0], dq_s.at[d, 0], dq_r.at[d, 0], owner(d, 0)).start()

        to_seq(dq_out.at[d, 1], dq_in.at[d, 1], dq_s.at[d, 1], dq_r.at[d, 1], owner(d, 1)).start()
        return carry

    lax.fori_loop(0, 4, grad_step, 0)

    for dy in (1, 0):
        for dz in (1, 0):
            for cc in (1, 0):
                n = dy * 4 + dz * 2 + cc
                dkv_out[dy, dz, cc, 0] = (dka[n * 128:(n + 1) * 128] * SCALE).astype(BF)
                dkv_out[dy, dz, cc, 1] = dva[n * 128:(n + 1) * 128].astype(BF)
                if n:
                    go(to_seq(dkv_out.at[dy, dz, cc], dkv_in.at[dy, dz, cc], dkv_s.at[dy, dz, cc],
                              dkv_r.at[dy, dz, cc], device(dy, dz, cc)))

    for cc in range(2):
        value = None
        for d in range(4):
            if cc or d:
                arrived(dq_in, dq_r, d, cc)
                part = dq_in[d, cc].astype(F32)
            else:
                part = dq_out[0, 0].astype(F32)
            value = part if value is None else value + part
        res[0, :, cols(cc)] = (value * SCALE).astype(BF)
    for cc in range(2):
        values = [dka[0:128] * SCALE, dva[0:128]] if cc == 0 else [None, None]
        for dy in range(2):
            for dz in range(2):
                if cc or dy or dz:
                    arrived(dkv_in, dkv_r, dy, dz, cc)
                    for a in range(2):
                        part = dkv_in[dy, dz, cc, a].astype(F32)
                        values[a] = part if values[a] is None else values[a] + part
        for a in range(2):
            res[1 + a, :, cols(cc)] = values[a].astype(BF)
    results = [pltpu.make_async_copy(res.at[n], ref, res_sem.at[n]) for n, ref in enumerate((dq_hbm, dk_hbm, dv_hbm))]
    for copy in results:
        copy.start()
    for copy in sent:
        copy.wait_send()
    for d in range(4):
        for cc in range(2):
            if cc or d:
                to_seq(ls_out.at[d, cc], ls_in.at[d, cc], ls_s.at[d, cc], ls_r.at[d, cc], owner(d, cc)).wait_send()
                to_seq(dq_out.at[d, cc], dq_in.at[d, cc], dq_s.at[d, cc], dq_r.at[d, cc], owner(d, cc)).wait_send()
    for copy in results:
        copy.wait()


def shards(queries, keys, values, attn_out, out_grad, out_weight, segment_ids):
    anywhere = pl.BlockSpec(memory_space=pl.ANY)
    dma = pltpu.SemaphoreType.DMA
    vmem = pltpu.VMEM
    out = jax.ShapeDtypeStruct((TOK, 2 * HD), BF)
    query_sems = [dma((4, 2))] * 2
    key_sems = [dma((2, 2, 2))] * 2
    return pl.pallas_call(
        kernel,
        out_shape=(out, out, out),
        in_specs=[anywhere] * 7,
        out_specs=(anywhere, anywhere, anywhere),
        scratch_shapes=[
            vmem((4, 2, TOK, HD), BF),
            vmem((2, 2, 2, TOK, HD), BF),
            vmem((2, 2, 2, TOK, HD), BF),
            vmem((4, 2, ROWS, HD), BF),
            vmem((8, TOK, 512), BF),
            vmem((4, 2, 8, 128), F32),
            vmem((4, 2, 8, 128), F32),
            vmem((256, 4096), BF),
            vmem((TOK, 2 * HD), BF),
            vmem((32, 128), jnp.int32),
            vmem((8, 128, 128), F32),
            vmem((HD, 1024), BF),
            vmem((4, 1024, 256), F32),
            vmem((4, 8, 256), F32),
            vmem((TOK, 2 * HD), BF),
            vmem((2, ROWS, HD), BF),
            vmem((1024, HD), F32),
            vmem((1024, HD), F32),
            vmem((4, 2, TOK, HD), BF),
            vmem((TOK, HD), F32),
            vmem((4, 2, TOK, HD), BF),
            vmem((2, 2, 2, 2, TOK, HD), BF),
            vmem((2, 2, 2, 2, TOK, HD), BF),
            vmem((3, TOK, 2 * HD), BF),
            dma, dma, dma, dma, dma((3,)), dma((3,)),
            *query_sems, *key_sems, *key_sems, *query_sems, dma((8,)), dma((8,)),
            *query_sems, *query_sems, *key_sems,
        ],
        compiler_params=pltpu.CompilerParams(
            collective_id=0, has_side_effects=True, vmem_limit_bytes=40 * 1024 * 1024),
    )(queries, keys, values, attn_out, out_grad, out_weight, segment_ids.reshape(32, 128))


def solution(mesh):
    return jax.shard_map(
        shards,
        mesh=mesh,
        in_specs=(
            P("seq", "head"),
            P("seq", "head"),
            P("seq", "head"),
            P("seq", "head"),
            P("seq", "head"),
            P("head", None),
            P(),
        ),
        out_specs=(P("seq", "head"), P("seq", "head"), P("seq", "head")),
        check_vma=False,
    )
```

time: 501 us -> 56.8 us (0.11); the launches traced: 494 us -> 56.5 us
  waiting for transfers between devices: 382 us -> 0 us
  Pallas kernels: 0 us -> 47.3 us
  matrix products: 36 us -> 0 us
  local copies, waits for them, and re-layouts: 33.1 us -> 8.45 us
  starting transfers between devices: 20.9 us -> 0 us
  between operations: 14.2 us -> 0.66 us
  other arithmetic: 5.27 us -> 0 us
    ppermute x126 -> x0, waiting for transfers between devices: 264 us -> none  [shifted(): return lax.ppermute(block, axis, route)]
    all_gather x2 -> x0, waiting for transfers between devices: 117 us -> none  [the longest x1 82.7 us: shards(): lax.all_gather(keys, 'seq', axis=0, tiled=True)]
    pallas_call x0 -> x1, Pallas kernels: none -> 47.3 us  [shards(): pl.pallas_call(kernel, out_shape=(out, out, out), in_specs=[anywhere] * 7...]
    dot_general x162 -> x0, matrix products: 36 us -> none  [the longest x32 7.01 us: tile_grads(): jnp.einsum('hqk,qhd->khd', score_low, query_part, preferred_element_type=...]
    dynamic_slice x32 -> x0, local copies, waits for them, and re-layouts: 24.5 us -> none  [advance(): lax.dynamic_slice_in_dim(segment_ids, anchor * tok_rows, tok_rows)]
    ppermute x126 -> x0, starting transfers between devices: 20.8 us -> none  [shifted(): return lax.ppermute(block, axis, route)]
  transfers between devices with their start and end apart: 128 -> 0, of which waited for: 125 -> 0; matrix products, arithmetic and copies ran while one was open for 14% -> 0% of each run, Pallas kernels for 0% -> 0%
where the time goes in v2:
time: 56.8 us; the launch traced here: 56.5 us
  Pallas kernels  47.3 us (83%)
  local copies, waits for them, and re-layouts  8.45 us (15%)
  between operations  0.66 us (1%)
    pallas_call x1, Pallas kernels, shards(): pl.pallas_call(kernel, out_shape=(out, out, out), in_specs=[anywhere] * 7...  47.3 us
    unnamed x17, local copies, waits for them, and re-layouts  8.45 us

profile of v2, /device:TPU:1, one launch (start us, length us, event | category | flops | bytes accessed | tf_op | source)
XLA Modules:
  0.0 56.5 jit_solution(1656668276465838949)
XLA Ops:
  0.6 0.0 copy-start
  0.6 1.6 %copy-done = bf16[256,4096]{1,0:T(8,128)(2,1)S(1)} copy-done((bf16[256,4096]{1,0:T(8,128)(2,1)S(1)}, bf16[256,4096]{1,0:T(8,128)(2,1)}, u32[]{:S(2)}) %copy-start) | copy-done | bytes 2097176
  2.2 0.0 copy-start.1
  2.2 0.9 %copy-done.1 = bf16[128,512]{1,0:T(8,128)(2,1)S(1)} copy-done((bf16[128,512]{1,0:T(8,128)(2,1)S(1)}, bf16[128,512]{1,0:T(8,128)(2,1)}, u32[]{:S(2)}) %copy-start.1) | copy-done | bytes 131096
  3.1 0.0 copy-start.2
  3.1 0.8 %copy-done.2 = bf16[128,256]{1,0:T(8,128)(2,1)S(1)} copy-done((bf16[128,256]{1,0:T(8,128)(2,1)S(1)}, bf16[128,256]{1,0:T(8,128)(2,1)}, u32[]{:S(2)}) %copy-start.2) | copy-done | bytes 65560
  4.0 0.0 copy-start.3
  4.0 0.8 %copy-done.3 = bf16[128,256]{1,0:T(8,128)(2,1)S(1)} copy-done((bf16[128,256]{1,0:T(8,128)(2,1)S(1)}, bf16[128,256]{1,0:T(8,128)(2,1)}, u32[]{:S(2)}) %copy-start.3) | copy-done | bytes 65560
  4.8 0.0 copy-start.4
  4.8 0.8 %copy-done.4 = bf16[128,256]{1,0:T(8,128)(2,1)S(1)} copy-done((bf16[128,256]{1,0:T(8,128)(2,1)S(1)}, bf16[128,256]{1,0:T(8,128)(2,1)}, u32[]{:S(2)}) %copy-start.4) | copy-done | bytes 65560
  5.6 0.0 copy-start.5
  5.7 0.8 %copy-done.5 = bf16[128,256]{1,0:T(8,128)(2,1)S(1)} copy-done((bf16[128,256]{1,0:T(8,128)(2,1)S(1)}, bf16[128,256]{1,0:T(8,128)(2,1)}, u32[]{:S(2)}) %copy-start.5) | copy-done | bytes 65560
  6.5 0.0 copy-start.6
  6.5 0.7 %copy-done.6 = s32[4096]{0:T(1024)S(1)} copy-done((s32[4096]{0:T(1024)S(1)}, s32[4096]{0:T(1024)}, u32[]{:S(2)}) %copy-start.6) | copy-done | bytes 16408
  7.2 47.3 %shard_map.94 = (bf16[128,256]{1,0:T(8,128)(2,1)S(1)}, bf16[128,256]{1,0:T(8,128)(2,1)S(1)}, bf16[128,256]{1,0:T(8,128)(2,1)S(1)}) custom-call(bf16[128,256]{1,0:T(8,128)(2,1)S(1)} %copy-done.2, bf16[128,256]{1,0:T(8,128)(2,1)S(1)} %copy-done.3, bf16[128,256]{1,0:T(8,128)(2,1)S(1)} %copy-done.4, bf16[128,256]{1,0:T(8,128)(2,1)S(1)} %copy-done.5, ...), custom_call_target="tpu_custom_call" | custom-call | tf_op jit(solution)/shard_map/pallas_call | solution.py:338
  54.6 0.6 %copy.13 = bf16[128,256]{1,0:T(8,128)(2,1)} copy(bf16[128,256]{1,0:T(8,128)(2,1)S(1)} %get-tuple-element.6) | data formatting | bytes 131072
  55.2 0.6 %copy.14 = bf16[128,256]{1,0:T(8,128)(2,1)} copy(bf16[128,256]{1,0:T(8,128)(2,1)S(1)} %get-tuple-element.7) | data formatting | bytes 131072
  55.8 0.6 %copy.15 = bf16[128,256]{1,0:T(8,128)(2,1)} copy(bf16[128,256]{1,0:T(8,128)(2,1)S(1)} %get-tuple-element.8) | data formatting | bytes 131072
Async XLA Ops:
  0.6 1.6 %copy-start = (bf16[256,4096]{1,0:T(8,128)(2,1)S(1)}, bf16[256,4096]{1,0:T(8,128)(2,1)}, u32[]{:S(2)}) copy-start(bf16[256,4096]{1,0:T(8,128)(2,1)} %w_hbm.1) | copy-start | bytes 6291460
  2.2 0.9 %copy-start.1 = (bf16[128,512]{1,0:T(8,128)(2,1)S(1)}, bf16[128,512]{1,0:T(8,128)(2,1)}, u32[]{:S(2)}) copy-start(bf16[128,512]{1,0:T(8,128)(2,1)} %og_hbm.1) | copy-start | bytes 393220
  3.1 0.8 %copy-start.2 = (bf16[128,256]{1,0:T(8,128)(2,1)S(1)}, bf16[128,256]{1,0:T(8,128)(2,1)}, u32[]{:S(2)}) copy-start(bf16[128,256]{1,0:T(8,128)(2,1)} %q_hbm.1) | copy-start | bytes 196612
  4.0 0.8 %copy-start.3 = (bf16[128,256]{1,0:T(8,128)(2,1)S(1)}, bf16[128,256]{1,0:T(8,128)(2,1)}, u32[]{:S(2)}) copy-start(bf16[128,256]{1,0:T(8,128)(2,1)} %k_hbm.1) | copy-start | bytes 196612
  4.8 0.8 %copy-start.4 = (bf16[128,256]{1,0:T(8,128)(2,1)S(1)}, bf16[128,256]{1,0:T(8,128)(2,1)}, u32[]{:S(2)}) copy-start(bf16[128,256]{1,0:T(8,128)(2,1)} %v_hbm.1) | copy-start | bytes 196612
  5.6 0.8 %copy-start.5 = (bf16[128,256]{1,0:T(8,128)(2,1)S(1)}, bf16[128,256]{1,0:T(8,128)(2,1)}, u32[]{:S(2)}) copy-start(bf16[128,256]{1,0:T(8,128)(2,1)} %o_hbm.1) | copy-start | bytes 196612
  6.5 0.7 %copy-start.6 = (s32[4096]{0:T(1024)S(1)}, s32[4096]{0:T(1024)}, u32[]{:S(2)}) copy-start(s32[4096]{0:T(1024)} %param.13) | copy-start | bytes 49156

commit v3 on v2

v3 whole, which is shorter than its diff:
```python
import jax
import jax.numpy as jnp
from jax import lax
from jax.experimental import pallas as pl
from jax.experimental.pallas import tpu as pltpu
from jax.sharding import PartitionSpec as P

HD = 128
TOK = 128
EXTRA = 16
HALF = TOK // 2
ROWS = HALF + EXTRA
SCALE = HD ** -0.5
LOG2E = 1.4426950408889634
MASKED = -1e30
FLOOR = -1e29
MESH = pl.DeviceIdType.MESH
BF = jnp.bfloat16
F32 = jnp.float32

SEQ_PEERS = (
    (0, -1, 0), (0, 1, 0), (0, 2, 0), (0, -2, 0), (0, -3, 0), (0, 3, 0),
    (0, 0, 1), (0, 1, 1), (0, -1, 1), (0, 3, 1), (0, -3, 1), (0, -2, 1),
    (1, 0, 0), (1, 1, 0), (1, 0, 1), (1, 1, 1), (1, -1, 1),
)
KEY_SLOTS = tuple((dy, dz, cc) for dy in range(2) for dz in range(2) for cc in range(2))
HEAD_PEERS = ((1, 0), (0, 1), (0, 2), (0, 3))
QUERY_STEPS = ((0, -1, 2, -3), (0, 1, -2, 3))
SHARE_STEPS = tuple(tuple(-d + QUERY_STEPS[d % 2][e] for e in range(4)) for d in range(4))


def dot_nt(a, b):
    return lax.dot_general(a, b, (((1,), (1,)), ((), ())), preferred_element_type=F32)


def dot_nn(a, b):
    return lax.dot_general(a, b, (((1,), (0,)), ((), ())), preferred_element_type=F32)


def across(row):
    return jnp.broadcast_to(row, (128, 128)).T


def pieces(x, count):
    out = []
    for _ in range(count):
        high = x.astype(BF).astype(F32)
        out.append(high)
        x = x - high
    return out


def stat_tile(rows):
    place = lax.broadcasted_iota(jnp.int32, (EXTRA, 128), 0)
    tile = jnp.zeros((EXTRA, 128), F32)
    for k, row in enumerate(rows):
        tile = jnp.where(place == k, jnp.broadcast_to(row, (EXTRA, 128)), tile)
    return tile.astype(BF)


def kernel(
    q_hbm, k_hbm, v_hbm, o_hbm, og_hbm, w_hbm, seg_hbm,
    dq_hbm, dk_hbm, dv_hbm,
    qb, kb, vb, gb, og_own, ogb, ls_in, ls_out, dl, dlt, w_ref, o_ref, seg_ref, segk, segq, kt, pb, mb, sh, ga,
    gstage, dka, dva, dqt, dq_out, dq_in, dkv_out, dkv_in, res,
    w_sem, o_sem, seg_sem, og_sem, own_sem, res_sem,
    q_s, q_r, k_s, k_r, v_s, v_r, g_s, g_r, og_s, og_r, ls_s, ls_r, dq_s, dq_r, dkv_s, dkv_r,
):
    seq = lax.axis_index("seq")
    head = lax.axis_index("head")
    y = seq // 16
    z = (seq // 2) % 8
    c = seq % 2
    ylo = head // 4
    x = head % 4
    sgn = 1 - 2 * ((z + c) % 2)

    def cols(other_head):
        h = 1 - c if other_head else c
        return pl.ds(pl.multiple_of(h * HD, HD), HD)

    def device(dy, steps, dc):
        yy = y + dy * (1 - 2 * y)
        return yy * 16 + ((z + 8 + sgn * steps) % 8) * 2 + (c + dc) % 2

    def to_seq(src, dst, ssem, rsem, target):
        return pltpu.make_async_remote_copy(
            src_ref=src, dst_ref=dst, send_sem=ssem, recv_sem=rsem,
            device_id={"seq": target}, device_id_type=MESH)

    def to_head(src, dst, ssem, rsem, target):
        return pltpu.make_async_remote_copy(
            src_ref=src, dst_ref=dst, send_sem=ssem, recv_sem=rsem,
            device_id={"head": target}, device_id_type=MESH)

    local = [
        pltpu.make_async_copy(k_hbm.at[:, cols(0)], kb.at[0, 0, 0], own_sem.at[0]),
        pltpu.make_async_copy(q_hbm.at[:, cols(0)], qb.at[0, 0], own_sem.at[1]),
        pltpu.make_async_copy(v_hbm.at[:, cols(0)], vb.at[0, 0, 0], own_sem.at[2]),
        pltpu.make_async_copy(og_hbm, og_own, og_sem),
        pltpu.make_async_copy(o_hbm, o_ref, o_sem),
        pltpu.make_async_copy(w_hbm, w_ref, w_sem),
    ]
    seg_copy = pltpu.make_async_copy(seg_hbm, seg_ref, seg_sem)
    seg_copy.start()
    for copy in local:
        copy.start()

    barrier = pltpu.get_barrier_semaphore()
    for peer in SEQ_PEERS:
        pl.semaphore_signal(barrier, inc=1, device_id={"seq": device(*peer)}, device_id_type=MESH)
    for dy, dx in HEAD_PEERS:
        peer = ((ylo + dy) % 2) * 4 + (x + dx) % 4
        pl.semaphore_signal(barrier, inc=1, device_id={"head": peer}, device_id_type=MESH)
    pl.semaphore_wait(barrier, len(SEQ_PEERS) + len(HEAD_PEERS))

    sent = []

    def go(copy):
        copy.start()
        sent.append(copy)

    def spread_keys(src, buf, ss, rs):
        for dy, dz, cc in ((1, 0, 0), (1, 0, 1), (0, 1, 0), (0, 1, 1), (0, 0, 1)):
            steps = (-dz if cc else dz)
            at = (dy, dz, cc)
            go(to_seq(src.at[:, cols(cc)], buf.at[at], ss.at[at], rs.at[at], device(dy, steps, cc)))

    def arrived(buf, rs, *at):
        to_seq(buf.at[at], buf.at[at], rs.at[at], rs.at[at], seq).wait_recv()

    def keys_on(buf, ss, rs):
        for cc in range(2):
            arrived(buf, rs, 1, 0, cc)
            go(to_seq(buf.at[1, 0, cc], buf.at[1, 1, cc], ss.at[1, 1, cc], rs.at[1, 1, cc], device(0, 1, 0)))

    def keys_arrived(buf, rs):
        for dy, dz, cc in ((0, 0, 1), (0, 1, 0), (0, 1, 1), (1, 1, 0), (1, 1, 1)):
            arrived(buf, rs, dy, dz, cc)

    def head_of(dy, dx):
        return ((ylo + dy) % 2) * 4 + (x + dx) % 4

    def rows_copy(src, slot, k, h, part, dy, dx):
        return to_head(src, ogb.at[slot, h, part], og_s.at[k, h, part], og_r.at[slot, h, part], head_of(dy, dx))

    def rows_to(*where):
        go(rows_copy(*where))

    def own_rows(h, part):
        n = h * 64 + part * 32
        return og_hbm.at[n:n + 32]

    def rows_x(h, part):
        for dx in (2, 1, 3):
            rows_to(own_rows(h, part), 4 - dx, dx, h, part, 0, dx)

    def rows_y(h, part):
        rows_to(own_rows(h, part), 4, 4, h, part, 1, 0)

    def rows_arrived(slot, h, part):
        at = (slot, h, part)
        to_head(ogb.at[at], ogb.at[at], og_s.at[at], og_r.at[at], head).wait_recv()

    def relay_x(h, dx):
        return rows_copy(ogb.at[4, h, 0], 8 - dx, 4 + dx, h, 0, 0, dx)

    def relay_y(h, dx):
        return rows_copy(ogb.at[dx, h, 1], 4 + dx, 4 + dx, h, 1, 1, 0)

    def rows_on_x(h):
        rows_arrived(4, h, 0)
        for dx in (2, 1, 3):
            relay_x(h, dx).start()

    def rows_on_y(h):
        for dx in (1, 3, 2):
            rows_arrived(dx, h, 1)
            relay_y(h, dx).start()

    def queries_to(*distances):
        for d in distances:
            for cc in range(2):
                if cc or d:
                    go(to_seq(q_hbm.at[:, cols(cc)], qb.at[d, cc], q_s.at[d, cc], q_r.at[d, cc],
                              device(0, QUERY_STEPS[cc][d], cc)))

    spread_keys(k_hbm, kb, k_s, k_r)
    rows_y(0, 0)
    rows_x(0, 1)
    rows_y(0, 1)
    rows_x(0, 0)
    rows_y(1, 0)
    rows_y(1, 1)
    rows_x(1, 1)
    queries_to(1, 0, 2, 3)
    seg_copy.wait()

    for dy in range(2):
        for dz in range(2):
            for cc in range(2):
                row = seg_ref[pl.ds(device(dy, dz, cc), 1), :].astype(F32)
                segk[dy * 4 + dz * 2 + cc] = across(row)

    for pair in range(2):
        rows = [seg_ref[pl.ds(device(0, -(2 * pair + dd), cc), 1), :].astype(F32) for dd in range(2) for cc in range(2)]
        for h in range(2):
            row = jnp.concatenate([r[:, h * 64:(h + 1) * 64] for r in rows], axis=1)
            segq[pair, h] = jnp.broadcast_to(row, (8, 256))

    def chunk(n):
        return n // 2, n % 2

    def blocks_arrived(buf, rs, pair, *lead):
        for dd in range(2):
            for cc in range(2):
                if dd or cc:
                    arrived(buf, rs, *lead, 2 * pair + dd, cc)
                else:
                    @pl.when(pair > 0)
                    def _():
                        arrived(buf, rs, *lead, 2 * pair, 0)

    def owner(d, cc):
        return device(0, -d, cc)

    def queries(pair, h):
        rows = pl.ds(pl.multiple_of(h * 64, 64), 64)
        return jnp.concatenate([qb[2 * pair + dd, cc, rows] for dd in range(2) for cc in range(2)], axis=0)

    mb[...] = jnp.full(mb.shape, FLOOR, F32)

    def scores(pair, dy):
        def one(h, carry):
            quer = queries(pair, h)
            row = segq[pair, h][0:1]
            top = mb[pair, h]
            for dz in range(2):
                n = 2 * dy + dz
                s = dot_nt(kb[dy, dz].reshape(256, HD), quer)
                seg = segk[2 * n:2 * n + 2].reshape(256, 128)
                s = jnp.where(jnp.concatenate([seg, seg], axis=1) == row, s, MASKED)
                pb[pair, h, n * 256:(n + 1) * 256] = s
                top = jnp.maximum(top, jnp.max(s.reshape(32, 8, 256), axis=0))
            mb[pair, h] = top
            return carry

        lax.fori_loop(0, 2, one, 0)

    for copy in local[:3]:
        copy.wait()
    rows_on_x(0)
    rows_on_y(0)
    rows_x(1, 0)
    keys_on(kb, k_s, k_r)
    for at in ((0, 0, 1), (0, 1, 0), (0, 1, 1)):
        arrived(kb, k_r, *at)
    blocks_arrived(qb, q_r, 0)
    scores(0, 0)
    rows_on_x(1)
    rows_on_y(1)
    spread_keys(v_hbm, vb, v_s, v_r)
    blocks_arrived(qb, q_r, 1)
    scores(1, 0)
    for cc in range(2):
        arrived(kb, k_r, 1, 1, cc)
    scores(0, 1)
    scores(1, 1)

    def share_copy(d, e):
        return to_seq(ls_out.at[d], ls_in.at[e, d], ls_s.at[d, e], ls_r.at[e, d], device(0, SHARE_STEPS[d][e], 0))

    for pair in range(2):
        def sum_step(h, carry):
            top = jnp.max(mb[pair, h], axis=0, keepdims=True)
            total = jnp.zeros((8, 256), F32)
            for n in range(4):
                p = jnp.exp2((pb[pair, h, n * 256:(n + 1) * 256] - top) * (SCALE * LOG2E))
                pb[pair, h, n * 256:(n + 1) * 256] = p
                total = total + jnp.sum(p.reshape(32, 8, 256), axis=0)
            total = jnp.sum(total, axis=0, keepdims=True)
            mb[pair, h] = jnp.broadcast_to(top * SCALE, (8, 256))
            logs = jnp.where(total > 0.0, top * SCALE + jnp.log(jnp.maximum(total, 1e-37)), MASKED)
            sh[pair, h] = jnp.broadcast_to(logs, (8, 256))
            return carry

        lax.fori_loop(0, 2, sum_step, 0)
        for dd in range(2):
            d = 2 * pair + dd
            for cc in range(2):
                n = (dd * 2 + cc) * 64
                ls_out[d, cc:cc + 1] = jnp.concatenate([sh[pair, 0][0:1, n:n + 64], sh[pair, 1][0:1, n:n + 64]], axis=1)
            for e in range(4):
                if e != d:
                    go(share_copy(d, e))
    for copy in local[3:]:
        copy.wait()

    def make_grad(h):
        acc = None
        for slot in (0, 4, 1, 3, 2, 5, 7, 6):
            block = ((ylo + slot // 4) % 2) * 4 + (x + slot) % 4
            for part in range(2):
                if slot and (slot, part) not in ((4, 0), (1, 1), (2, 1), (3, 1)):
                    rows_arrived(slot, h, part)
            rows = ogb[slot, h].reshape(HALF, 512) if slot else og_own[h * 64:(h + 1) * 64]
            term = dot_nt(rows, w_ref[:, pl.ds(pl.multiple_of(block * 512, 512), 512)])
            acc = term if acc is None else acc + term
        ga[h] = acc.astype(BF)
        for cc in range(2):
            grad = ga[h, :, cols(cc)]
            prod = grad.astype(F32) * o_ref[h * 64:(h + 1) * 64, cols(cc)].astype(F32)
            prod = jnp.concatenate([prod, jnp.zeros((64, HD), F32)], axis=0)
            gstage[h, cc, 0:HALF] = grad
            dl[h, cc] = jnp.broadcast_to(jnp.sum(prod.T, axis=0, keepdims=True), (8, 128))

    def send_grad(h):
        for cc in range(2):
            gstage[h, cc, HALF:ROWS] = stat_tile(pieces(dl[h, cc][0:1], 2))
        for d in (3, 2, 1, 0):
            for cc in range(2):
                if cc or d:
                    go(to_seq(gstage.at[h, cc], gb.at[h, d, cc], g_s.at[h, d, cc], g_r.at[h, d, cc],
                              device(0, QUERY_STEPS[cc][d], cc)))
        gb[h, 0, 0] = gstage[h, 0]

    make_grad(0)
    send_grad(0)
    keys_on(vb, v_s, v_r)
    make_grad(1)
    send_grad(1)
    for n, (dy, dz, cc) in enumerate(KEY_SLOTS):
        kt[:, n * 128:(n + 1) * 128] = kb[dy, dz, cc].astype(F32).T.astype(BF)
    dka[...] = jnp.zeros(dka.shape, F32)
    dva[...] = jnp.zeros(dva.shape, F32)
    keys_arrived(vb, v_r)
    log_sums = []
    for d in range(4):
        parts = [ls_out[d]]
        for e in range(4):
            if e != d:
                arrived(ls_in, ls_r, d, e)
                parts.append(ls_in[d, e])
        top = jnp.maximum(jnp.maximum(parts[0], parts[1]), jnp.maximum(parts[2], parts[3]))
        total = sum(jnp.exp(part - top) for part in parts)
        log_sums.append(top + jnp.log(total))
    for pair in range(2):
        for h in range(2):
            row = jnp.concatenate([
                log_sums[2 * pair + dd][cc:cc + 1, h * 64:(h + 1) * 64] for dd in range(2) for cc in range(2)], axis=1)
            sh[pair, h] = jnp.exp(mb[pair, h] - row)

    places = [(d, cc) for d in range(4) for cc in range(2)]

    def grad_step(i, carry):
        h, n = i // 4, 3 - i % 4
        dy, dz = n // 2, n % 2

        @pl.when(n == 3)
        def _():
            for d, cc in places:
                if d or cc:
                    arrived(gb, g_r, h, d, cc)
            dqt[...] = jnp.zeros(dqt.shape, F32)
            deltas = []
            for d, cc in places:
                stats = gb[h, d, cc, HALF:ROWS].astype(F32)
                deltas.append((stats[0:1] + stats[1:2])[:, 0:64])
            dlt[...] = jnp.broadcast_to(jnp.concatenate(deltas, axis=1), (8, 512))

        quer = jnp.concatenate([queries(pair, h) for pair in range(2)], axis=0)
        grad = jnp.concatenate([gb[h, d, cc, 0:HALF] for d, cc in places], axis=0)
        deltas = dlt[0:1]
        part = pl.ds(pl.multiple_of(n * 256, 256), 256)
        p = jnp.concatenate([pb[pair, h, part] * sh[pair, h][0:1] for pair in range(2)], axis=1)
        dva[part] += dot_nn(p.astype(BF), grad)
        dp = dot_nt(vb[dy, dz].reshape(256, HD), grad)
        ds = (p * (dp - deltas)).astype(BF)
        dka[part] += dot_nn(ds, quer)
        dqt[...] += dot_nn(kt[:, part], ds)

        @pl.when(h == 1)
        def _():
            for cc in range(2):
                rows = pl.ds(pl.multiple_of(n * 256 + cc * 128, 128), 128)
                dkv_out[dy, dz, cc, 0] = (dka[rows] * SCALE).astype(BF)
                dkv_out[dy, dz, cc, 1] = dva[rows].astype(BF)
                if cc:
                    dkv_copy(dy, dz, 1).start()
                else:
                    @pl.when(n > 0)
                    def _():
                        dkv_copy(dy, dz, 0).start()

        @pl.when(n == 0)
        def _():
            for d in (3, 2, 1, 0):
                tokens = dqt[:, d * 128:(d + 1) * 128].T.astype(BF)
                for cc in range(2):
                    dq_out[h, d, cc] = tokens[cc * 64:(cc + 1) * 64]
                    if d or cc:
                        dq_copy(h, d, cc).start()

        return carry

    def dq_copy(h, d, cc):
        return to_seq(dq_out.at[h, d, cc], dq_in.at[h, d, cc], dq_s.at[h, d, cc], dq_r.at[h, d, cc], owner(d, cc))

    def dkv_copy(dy, dz, cc):
        return to_seq(dkv_out.at[dy, dz, cc], dkv_in.at[dy, dz, cc], dkv_s.at[dy, dz, cc], dkv_r.at[dy, dz, cc],
                      device(dy, dz, cc))

    lax.fori_loop(0, 8, grad_step, 0)

    for h in range(2):
        for cc in range(2):
            value = None
            for d in range(4):
                if cc or d:
                    arrived(dq_in, dq_r, h, d, cc)
                    part = dq_in[h, d, cc].astype(F32)
                else:
                    part = dq_out[h, 0, 0].astype(F32)
                value = part if value is None else value + part
            res[0, h * 64:(h + 1) * 64, cols(cc)] = (value * SCALE).astype(BF)
    for cc in range(2):
        values = [dka[0:128] * SCALE, dva[0:128]] if cc == 0 else [None, None]
        for dy in range(2):
            for dz in range(2):
                if cc or dy or dz:
                    arrived(dkv_in, dkv_r, dy, dz, cc)
                    for a in range(2):
                        part = dkv_in[dy, dz, cc, a].astype(F32)
                        values[a] = part if values[a] is None else values[a] + part
        for a in range(2):
            res[1 + a, :, cols(cc)] = values[a].astype(BF)
    results = [pltpu.make_async_copy(res.at[n], ref, res_sem.at[n]) for n, ref in enumerate((dq_hbm, dk_hbm, dv_hbm))]
    for copy in results:
        copy.start()
    relays = [relay(h, dx) for h in range(2) for relay in (relay_x, relay_y) for dx in (1, 2, 3)]
    for copy in sent + relays:
        copy.wait_send()
    for d, cc in places:
        if cc or d:
            for h in range(2):
                dq_copy(h, d, cc).wait_send()
    for dy, dz, cc in KEY_SLOTS[1:]:
        dkv_copy(dy, dz, cc).wait_send()
    for copy in results:
        copy.wait()


def deliver(a_ref, b_ref, c_ref, dq_ref, dk_ref, dv_ref):
    dq_ref[...] = a_ref[...]
    dk_ref[...] = b_ref[...]
    dv_ref[...] = c_ref[...]


def shards(queries, keys, values, attn_out, out_grad, out_weight, segment_ids):
    anywhere = pl.BlockSpec(memory_space=pl.ANY)
    dma = pltpu.SemaphoreType.DMA
    vmem = pltpu.VMEM
    out = jax.ShapeDtypeStruct((TOK, 2 * HD), BF)
    query_sems = [dma((4, 2))] * 2
    key_sems = [dma((2, 2, 2))] * 2
    chunk_sems = [dma((2, 4, 2))] * 2
    held = pl.pallas_call(
        kernel,
        out_shape=(out, out, out),
        in_specs=[anywhere] * 7,
        out_specs=(anywhere, anywhere, anywhere),
        scratch_shapes=[
            vmem((4, 2, TOK, HD), BF),
            vmem((2, 2, 2, TOK, HD), BF),
            vmem((2, 2, 2, TOK, HD), BF),
            vmem((2, 4, 2, ROWS, HD), BF),
            vmem((TOK, 512), BF),
            vmem((8, 2, 2, 32, 512), BF),
            vmem((4, 4, 2, 128), F32),
            vmem((4, 2, 128), F32),
            vmem((2, 2, 8, 128), F32),
            vmem((8, 512), F32),
            vmem((256, 4096), BF),
            vmem((TOK, 2 * HD), BF),
            vmem((32, 128), jnp.int32),
            vmem((8, 128, 128), F32),
            vmem((2, 2, 8, 256), F32),
            vmem((HD, 1024), BF),
            vmem((2, 2, 1024, 256), F32),
            vmem((2, 2, 8, 256), F32),
            vmem((2, 2, 8, 256), F32),
            vmem((2, HALF, 2 * HD), BF),
            vmem((2, 2, ROWS, HD), BF),
            vmem((1024, HD), F32),
            vmem((1024, HD), F32),
            vmem((HD, 512), F32),
            vmem((2, 4, 2, HALF, HD), BF),
            vmem((2, 4, 2, HALF, HD), BF),
            vmem((2, 2, 2, 2, TOK, HD), BF),
            vmem((2, 2, 2, 2, TOK, HD), BF),
            vmem((3, TOK, 2 * HD), BF),
            dma, dma, dma, dma, dma((3,)), dma((3,)),
            *query_sems, *key_sems, *key_sems, *chunk_sems, dma((8, 2, 2)), dma((8, 2, 2)),
            dma((4, 4)), dma((4, 4)), *chunk_sems, *key_sems,
        ],
        compiler_params=pltpu.CompilerParams(
            collective_id=0, has_side_effects=True, vmem_limit_bytes=60 * 1024 * 1024),
    )(queries, keys, values, attn_out, out_grad, out_weight, segment_ids.reshape(32, 128))
    return pl.pallas_call(
        deliver,
        out_shape=(out, out, out),
        in_specs=[pl.BlockSpec(memory_space=pltpu.VMEM)] * 3,
        out_specs=(pl.BlockSpec(memory_space=pltpu.VMEM),) * 3,
        name="deliver_call",
    )(*held)


def solution(mesh):
    return jax.shard_map(
        shards,
        mesh=mesh,
        in_specs=(
            P("seq", "head"),
            P("seq", "head"),
            P("seq", "head"),
            P("seq", "head"),
            P("seq", "head"),
            P("head", None),
            P(),
        ),
        out_specs=(P("seq", "head"), P("seq", "head"), P("seq", "head")),
        check_vma=False,
    )
```

time: 56.8 us -> 44.8 us (0.79)
  local copies, waits for them, and re-layouts: 8.45 us -> 0 us
  Pallas kernels: 47.3 us -> 44 us
    unnamed x17 -> x0, local copies, waits for them, and re-layouts: 8.45 us -> none
    pallas_call x1, Pallas kernels: 47.3 us -> 42.4 us  [shards(): pl.pallas_call(kernel, out_shape=(out, out, out), in_specs=[anywhere] * 7...]
    pallas_call x0 -> x1, Pallas kernels: none -> 1.58 us  [shards(): pl.pallas_call(deliver, out_shape=(out, out, out), in_specs=[pl.BlockSpec...]
where the time goes in v3:
time: 44.8 us; the launch traced here: 44.7 us
  Pallas kernels  44 us (98%)
  between operations  0.64 us (1%)
    pallas_call x1, Pallas kernels, shards(): pl.pallas_call(kernel, out_shape=(out, out, out), in_specs=[anywhere] * 7...  42.4 us
    pallas_call x1, Pallas kernels, shards(): pl.pallas_call(deliver, out_shape=(out, out, out), in_specs=[pl.BlockSpec...  1.58 us

profile of v3, /device:TPU:1, one launch (start us, length us, event | category | flops | bytes accessed | tf_op | source)
XLA Modules:
  0.0 44.7 jit_solution(4728527402129763437)
XLA Ops:
  0.6 42.4 %shard_map.94 = (bf16[128,256]{1,0:T(8,128)(2,1)}, bf16[128,256]{1,0:T(8,128)(2,1)}, bf16[128,256]{1,0:T(8,128)(2,1)}) custom-call(bf16[128,256]{1,0:T(8,128)(2,1)} %q_hbm.1, bf16[128,256]{1,0:T(8,128)(2,1)} %k_hbm.1, bf16[128,256]{1,0:T(8,128)(2,1)} %v_hbm.1, bf16[128,256]{1,0:T(8,128)(2,1)} %o_hbm.1, bf16[128,512]{1,0:T(8,128)(2,1)} %og_hbm.1, ...), custom_call_target="tpu_custom_call" | custom-call | tf_op jit(solution)/shard_map/pallas_call | solution.py:467
  43.1 1.6 %deliver_call.1 = (bf16[128,256]{1,0:T(8,128)(2,1)}, bf16[128,256]{1,0:T(8,128)(2,1)}, bf16[128,256]{1,0:T(8,128)(2,1)}) custom-call(bf16[128,256]{1,0:T(8,128)(2,1)} %get-tuple-element.6.a_ref, bf16[128,256]{1,0:T(8,128)(2,1)} %get-tuple-element.7.b_ref, bf16[128,256]{1,0:T(8,128)(2,1)} %get-tuple-element.8.c_ref), custom_call_target="tpu_custom_call" | custom-call | tf_op jit(solution)/shard_map/deliver_call/pallas_call | solution.py:509

commit v4 on v3

v4 whole, which is shorter than its diff:
```python
import jax
import jax.numpy as jnp
from jax import lax
from jax.experimental import pallas as pl
from jax.experimental.pallas import tpu as pltpu
from jax.sharding import PartitionSpec as P

HD = 128
TOK = 128
EXTRA = 16
SPLIT = 64
PARTS = (slice(0, SPLIT), slice(SPLIT, TOK))
ROWS = TOK + EXTRA
SCALE = HD ** -0.5
LOG2E = 1.4426950408889634
MASKED = -1e30
FLOOR = -1e29
MESH = pl.DeviceIdType.MESH
BF = jnp.bfloat16
F32 = jnp.float32

SEQ_PEERS = (
    (0, -1, 0), (0, 1, 0), (0, 2, 0), (0, -2, 0), (0, -3, 0), (0, 3, 0),
    (0, 0, 1), (0, 1, 1), (0, -1, 1), (0, 3, 1), (0, -3, 1), (0, -2, 1),
    (1, 0, 0), (1, 1, 0), (1, 0, 1), (1, 1, 1), (1, -1, 1),
)
NEAR_FIRST = (1, 0, 2, 3)
KEY_SLOTS = tuple((dy, dz, cc) for dy in range(2) for dz in range(2) for cc in range(2))
HEAD_PEERS = ((1, 0), (0, 1), (0, 2), (0, 3))
QUERY_STEPS = ((0, -1, 2, -3), (0, 1, -2, 3))
SHARE_STEPS = tuple(tuple(-d + QUERY_STEPS[d % 2][e] for e in range(4)) for d in range(4))


def dot_nt(a, b):
    return lax.dot_general(a, b, (((1,), (1,)), ((), ())), preferred_element_type=F32)


def dot_nn(a, b):
    return lax.dot_general(a, b, (((1,), (0,)), ((), ())), preferred_element_type=F32)


def across(row):
    return jnp.broadcast_to(row, (128, 128)).T


def pieces(x, count):
    out = []
    for _ in range(count):
        high = x.astype(BF).astype(F32)
        out.append(high)
        x = x - high
    return out


def stat_tile(rows):
    place = lax.broadcasted_iota(jnp.int32, (EXTRA, 128), 0)
    tile = jnp.zeros((EXTRA, 128), F32)
    for k, row in enumerate(rows):
        tile = jnp.where(place == k, jnp.broadcast_to(row, (EXTRA, 128)), tile)
    return tile.astype(BF)


def kernel(
    q_hbm, k_hbm, v_hbm, o_hbm, og_hbm, w_hbm, seg_hbm,
    dq_in, dkv_in,
    qb, kb, vb, gb, og_own, ogb, ls_in, ls_out, w_ref, o_ref, seg_ref, segk, segq, kt, pb, mb, sh, lb, ga,
    gstage, dka, dva, dqt, dlt, dq_out, dkv_out,
    w_sem, o_sem, seg_sem, og_sem, own_sem, res_sem,
    q_s, q_r, k_s, k_r, v_s, v_r, g_s, g_r, og_s, og_r, ls_s, ls_r, dq_s, dq_r, dkv_s, dkv_r,
):
    seq = lax.axis_index("seq")
    head = lax.axis_index("head")
    y = seq // 16
    z = (seq // 2) % 8
    c = seq % 2
    ylo = head // 4
    x = head % 4
    sgn = 1 - 2 * ((z + c) % 2)

    def cols(other_head):
        h = 1 - c if other_head else c
        return pl.ds(pl.multiple_of(h * HD, HD), HD)

    def place(dy, steps, dc):
        yy = y + dy * (1 - 2 * y)
        return yy * 16 + ((z + 8 + sgn * steps) % 8) * 2 + (c + dc) % 2

    places_at = {(dy, steps, dc): place(dy, steps, dc) for dy in range(2) for steps in range(-5, 4) for dc in range(2)}

    def device(*where):
        return places_at[where] if all(isinstance(n, int) for n in where) else place(*where)

    def to_seq(src, dst, ssem, rsem, target):
        return pltpu.make_async_remote_copy(
            src_ref=src, dst_ref=dst, send_sem=ssem, recv_sem=rsem,
            device_id={"seq": target}, device_id_type=MESH)

    def to_head(src, dst, ssem, rsem, target):
        return pltpu.make_async_remote_copy(
            src_ref=src, dst_ref=dst, send_sem=ssem, recv_sem=rsem,
            device_id={"head": target}, device_id_type=MESH)

    local = [
        pltpu.make_async_copy(k_hbm.at[:, cols(0)], kb.at[0, 0, 0], own_sem.at[0]),
        pltpu.make_async_copy(q_hbm.at[:, cols(0)], qb.at[0, 0], own_sem.at[1]),
        pltpu.make_async_copy(v_hbm.at[:, cols(0)], vb.at[0, 0, 0], own_sem.at[2]),
        pltpu.make_async_copy(og_hbm, og_own, og_sem),
        pltpu.make_async_copy(o_hbm, o_ref, o_sem),
        pltpu.make_async_copy(w_hbm, w_ref, w_sem),
    ]
    seg_copy = pltpu.make_async_copy(seg_hbm, seg_ref, seg_sem)
    seg_copy.start()
    for copy in local:
        copy.start()

    barrier = pltpu.get_barrier_semaphore()
    for peer in SEQ_PEERS:
        pl.semaphore_signal(barrier, inc=1, device_id={"seq": device(*peer)}, device_id_type=MESH)
    for dy, dx in HEAD_PEERS:
        peer = ((ylo + dy) % 2) * 4 + (x + dx) % 4
        pl.semaphore_signal(barrier, inc=1, device_id={"head": peer}, device_id_type=MESH)
    pl.semaphore_wait(barrier, len(SEQ_PEERS) + len(HEAD_PEERS))

    sent = []

    def go(copy):
        copy.start()
        sent.append(copy)

    def spread_keys(src, buf, ss, rs):
        for dy, dz, cc in ((1, 0, 0), (1, 0, 1), (0, 1, 0), (0, 1, 1), (0, 0, 1)):
            steps = (-dz if cc else dz)
            at = (dy, dz, cc)
            go(to_seq(src.at[:, cols(cc)], buf.at[at], ss.at[at], rs.at[at], device(dy, steps, cc)))

    def arrived(buf, rs, *at):
        to_seq(buf.at[at], buf.at[at], rs.at[at], rs.at[at], seq).wait_recv()

    def keys_on(buf, ss, rs):
        for cc in range(2):
            arrived(buf, rs, 1, 0, cc)
            go(to_seq(buf.at[1, 0, cc], buf.at[1, 1, cc], ss.at[1, 1, cc], rs.at[1, 1, cc], device(0, 1, 0)))

    def spread_directly(src, buf, ss, rs, which):
        for dy, dz, cc in which:
            at = (dy, dz, cc)
            go(to_seq(src.at[:, cols(cc)], buf.at[at], ss.at[at], rs.at[at], device(dy, (-dz if cc else dz), cc)))

    def keys_arrived(buf, rs):
        for dy, dz, cc in ((0, 0, 1), (0, 1, 0), (0, 1, 1), (1, 1, 0), (1, 1, 1)):
            arrived(buf, rs, dy, dz, cc)

    heads_at = {(dy, dx): ((ylo + dy) % 2) * 4 + (x + dx) % 4 for dy in range(2) for dx in range(4)}

    def rows_copy(src, slot, k, part, dy, dx):
        return to_head(src, ogb.at[slot, PARTS[part]], og_s.at[k, part], og_r.at[slot, part], heads_at[dy, dx])

    def own_rows(part):
        return og_hbm.at[PARTS[part]]

    def rows_x(part):
        for dx in (2, 1, 3):
            go(rows_copy(own_rows(part), 4 - dx, dx, part, 0, dx))

    def rows_y(part):
        go(rows_copy(own_rows(part), 4, 4, part, 1, 0))

    def rows_arrived(slot, part):
        at = (slot, part)
        rows = ogb.at[slot, PARTS[part]]
        to_head(rows, rows, og_s.at[at], og_r.at[at], head).wait_recv()

    def rows_on_x():
        rows_arrived(4, 0)
        for dx in (2, 1, 3):
            go(rows_copy(ogb.at[4, PARTS[0]], 8 - dx, 4 + dx, 0, 0, dx))

    def rows_on_y():
        for dx in (1, 3, 2):
            rows_arrived(dx, 1)
            go(rows_copy(ogb.at[dx, PARTS[1]], 4 + dx, 4 + dx, 1, 1, 0))

    def queries_to(*distances):
        for d in distances:
            for cc in range(2):
                if cc or d:
                    go(to_seq(q_hbm.at[:, cols(cc)], qb.at[d, cc], q_s.at[d, cc], q_r.at[d, cc],
                              device(0, QUERY_STEPS[cc][d], cc)))

    rows_y(0)
    spread_directly(k_hbm, kb, k_s, k_r, KEY_SLOTS[1:])
    rows_x(1)
    rows_x(0)
    rows_y(1)
    queries_to(1, 0, 2, 3)
    spread_keys(v_hbm, vb, v_s, v_r)
    seg_copy.wait()

    for dy in range(2):
        for dz in range(2):
            for cc in range(2):
                row = seg_ref[pl.ds(device(dy, dz, cc), 1), :].astype(F32)
                segk[dy * 4 + dz * 2 + cc] = across(row)

    for pair in range(2):
        rows = [seg_ref[pl.ds(device(0, -(2 * pair + dd), cc), 1), :].astype(F32) for dd in range(2) for cc in range(2)]
        segq[pair] = jnp.broadcast_to(jnp.concatenate(rows, axis=1), (8, 512))

    def chunk(n):
        return n // 2, n % 2

    def blocks_arrived(buf, rs, pair, *lead):
        for dd in range(2):
            for cc in range(2):
                if dd or cc:
                    arrived(buf, rs, *lead, 2 * pair + dd, cc)
                else:
                    @pl.when(pair > 0)
                    def _():
                        arrived(buf, rs, *lead, 2 * pair, 0)

    def owner(d, cc):
        return device(0, -d, cc)

    def queries(pair):
        return qb[pl.ds(2 * pair, 2)].reshape(512, HD)

    mb[...] = jnp.full(mb.shape, FLOOR, F32)

    def scores(pair, dy):
        def one(dz, carry):
            n = 2 * dy + dz
            s = dot_nt(kb[dy, dz].reshape(256, HD), queries(pair))
            seg = segk[pl.ds(2 * n, 2)].reshape(256, 128)
            s = jnp.where(jnp.concatenate([seg] * 4, axis=1) == segq[pair][0:1], s, MASKED)
            pb[pair, pl.ds(pl.multiple_of(n * 256, 256), 256)] = s
            mb[pair] = jnp.maximum(mb[pair], jnp.max(s.reshape(32, 8, 512), axis=0))
            return carry

        lax.fori_loop(0, 2, one, 0)

    for copy in local[:3]:
        copy.wait()
    for at in ((0, 0, 1), (0, 1, 0), (0, 1, 1)):
        arrived(kb, k_r, *at)
    blocks_arrived(qb, q_r, 0)
    scores(0, 0)
    rows_on_x()
    rows_on_y()
    for cc in range(2):
        arrived(kb, k_r, 1, 0, cc)
        arrived(kb, k_r, 1, 1, cc)
    scores(0, 1)
    blocks_arrived(qb, q_r, 1)
    scores(1, 0)
    scores(1, 1)
    keys_on(vb, v_s, v_r)

    def share_copy(d, e):
        return to_seq(ls_out.at[d], ls_in.at[e, d], ls_s.at[d, e], ls_r.at[e, d], device(0, SHARE_STEPS[d][e], 0))

    def sums(pair):
        top = jnp.max(mb[pair], axis=0, keepdims=True)
        lb[...] = jnp.zeros(lb.shape, F32)

        def one(n, carry):
            part = pl.ds(pl.multiple_of(n * 256, 256), 256)
            p = jnp.exp2((pb[pair, part] - top) * (SCALE * LOG2E))
            pb[pair, part] = p
            lb[...] += jnp.sum(p.reshape(32, 8, 512), axis=0)
            return carry

        lax.fori_loop(0, 4, one, 0)
        total = jnp.sum(lb[...], axis=0, keepdims=True)
        mb[pair] = jnp.broadcast_to(top * SCALE, (8, 512))
        logs = jnp.where(total > 0.0, top * SCALE + jnp.log(jnp.maximum(total, 1e-37)), MASKED)
        for dd in range(2):
            d = 2 * pair + dd
            for cc in range(2):
                n = (dd * 2 + cc) * 128
                ls_out[d, cc:cc + 1] = logs[:, n:n + 128]
            for e in range(4):
                if e != d:
                    go(share_copy(d, e))

    sums(0)
    sums(1)
    for copy in local[3:]:
        copy.wait()

    acc = None
    for slot in (0, 4, 1, 3, 2, 5, 7, 6):
        block = heads_at[slot // 4, slot % 4]
        for part in range(2):
            if slot and (slot, part) not in ((4, 0), (1, 1), (2, 1), (3, 1)):
                rows_arrived(slot, part)
        rows = ogb[slot] if slot else og_own[...]
        term = dot_nt(rows, w_ref[:, pl.ds(pl.multiple_of(block * 512, 512), 512)])
        acc = term if acc is None else acc + term
    ga[...] = acc.astype(BF)
    for cc in range(2):
        grad = ga[:, cols(cc)]
        delta = jnp.sum((grad.astype(F32) * o_ref[:, cols(cc)].astype(F32)).T, axis=0, keepdims=True)
        gstage[cc, 0:TOK] = grad
        gstage[cc, TOK:ROWS] = stat_tile(pieces(delta, 2))

    def send_grad(*distances):
        for d in distances:
            for cc in range(2):
                if cc or d:
                    go(to_seq(gstage.at[cc], gb.at[d, cc], g_s.at[d, cc], g_r.at[d, cc],
                              device(0, QUERY_STEPS[cc][d], cc)))

    send_grad(1, 0)
    gb[0, 0] = gstage[0]
    send_grad(2, 3)
    for n, (dy, dz, cc) in enumerate(KEY_SLOTS):
        kt[:, n * 128:(n + 1) * 128] = kb[dy, dz, cc].astype(F32).T.astype(BF)
    dka[...] = jnp.zeros(dka.shape, F32)
    dva[...] = jnp.zeros(dva.shape, F32)
    keys_arrived(vb, v_r)
    log_sums = []
    for d in range(4):
        parts = [ls_out[d]]
        for e in range(4):
            if e != d:
                arrived(ls_in, ls_r, d, e)
                parts.append(ls_in[d, e])
        top = jnp.maximum(jnp.maximum(parts[0], parts[1]), jnp.maximum(parts[2], parts[3]))
        total = sum(jnp.exp(part - top) for part in parts)
        log_sums.append(top + jnp.log(total))
    for pair in range(2):
        row = jnp.concatenate([log_sums[2 * pair + dd][cc:cc + 1] for dd in range(2) for cc in range(2)], axis=1)
        sh[pair] = jnp.exp(mb[pair] - row)

    places = [(d, cc) for d in range(4) for cc in range(2)]

    def grad_step(i, carry):
        pair, n = i // 4, 3 - i % 4
        dy, dz = n // 2, n % 2

        @pl.when(n == 3)
        def _():
            blocks_arrived(gb, g_r, pair)
            dqt[...] = jnp.zeros(dqt.shape, F32)
            deltas = []
            for dd in range(2):
                for cc in range(2):
                    stats = gb[2 * pair + dd, cc, TOK:ROWS].astype(F32)
                    deltas.append(stats[0:1] + stats[1:2])
            dlt[...] = jnp.broadcast_to(jnp.concatenate(deltas, axis=1), (8, 512))

        quer = queries(pair)
        grad = gb[pl.ds(2 * pair, 2), :, 0:TOK].reshape(512, HD)
        part = pl.ds(pl.multiple_of(n * 256, 256), 256)
        p = pb[pair, part] * sh[pair][0:1]
        dva[part] += dot_nn(p.astype(BF), grad)
        dp = dot_nt(vb[dy, dz].reshape(256, HD), grad)
        ds = (p * (dp - dlt[0:1])).astype(BF)
        dka[part] += dot_nn(ds, quer)
        dqt[...] += dot_nn(kt[:, part], ds)

        @pl.when(pair == 1)
        def _():
            for cc in range(2):
                rows = pl.ds(pl.multiple_of(n * 256 + cc * 128, 128), 128)
                dkv_out[dy, dz, cc, 0] = (dka[rows] * SCALE).astype(BF)
                dkv_out[dy, dz, cc, 1] = dva[rows].astype(BF)
                if cc:
                    dkv_copy(dy, dz, 1).start()
                else:
                    @pl.when(n > 0)
                    def _():
                        dkv_copy(dy, dz, 0).start()

        @pl.when(n == 0)
        def _():
            for dd in (1, 0):
                d = 2 * pair + dd
                for cc in range(2):
                    k = (dd * 2 + cc) * 128
                    dq_out[d, cc] = dqt[:, k:k + 128].T.astype(BF)
                    if dd or cc:
                        dq_copy(d, cc).start()
                    else:
                        @pl.when(pair > 0)
                        def _():
                            dq_copy(d, 0).start()

        return carry

    def dq_copy(d, cc):
        return to_seq(dq_out.at[d, cc], dq_in.at[d, cc], dq_s.at[d, cc], dq_r.at[d, cc], owner(d, cc))

    def dkv_copy(dy, dz, cc):
        return to_seq(dkv_out.at[dy, dz, cc], dkv_in.at[dy, dz, cc], dkv_s.at[dy, dz, cc], dkv_r.at[dy, dz, cc],
                      device(dy, dz, cc))

    lax.fori_loop(0, 8, grad_step, 0)

    results = [
        pltpu.make_async_copy(dq_out.at[0, 0], dq_in.at[0, 0], res_sem.at[0]),
        pltpu.make_async_copy(dkv_out.at[0, 0, 0], dkv_in.at[0, 0, 0], res_sem.at[1]),
    ]
    for copy in results:
        copy.start()
    for copy in sent:
        copy.wait_send()
    for d, cc in places[1:]:
        dq_copy(d, cc).wait_send()
        arrived(dq_in, dq_r, d, cc)
    for at in KEY_SLOTS[1:]:
        dkv_copy(*at).wait_send()
        arrived(dkv_in, dkv_r, *at)
    for copy in results:
        copy.wait()


def deliver(dq_in, dkv_in, dq_ref, dk_ref, dv_ref):
    c = lax.axis_index("seq") % 2
    for cc in range(2):
        h = (c + cc) % 2
        cols = pl.ds(pl.multiple_of(h * HD, HD), HD)
        parts = [dq_in[d, cc].astype(F32) for d in range(4)]
        dq_ref[:, cols] = (((parts[0] + parts[1]) + (parts[2] + parts[3])) * SCALE).astype(BF)
        for a, ref in enumerate((dk_ref, dv_ref)):
            parts = [dkv_in[dy, dz, cc, a].astype(F32) for dy in range(2) for dz in range(2)]
            ref[:, cols] = ((parts[0] + parts[1]) + (parts[2] + parts[3])).astype(BF)


def shards(queries, keys, values, attn_out, out_grad, out_weight, segment_ids):
    anywhere = pl.BlockSpec(memory_space=pl.ANY)
    dma = pltpu.SemaphoreType.DMA
    vmem = pltpu.VMEM
    out = jax.ShapeDtypeStruct((TOK, 2 * HD), BF)
    query_sems = [dma((4, 2))] * 2
    key_sems = [dma((2, 2, 2))] * 2
    held = pl.pallas_call(
        kernel,
        out_shape=(
            jax.ShapeDtypeStruct((4, 2, TOK, HD), BF),
            jax.ShapeDtypeStruct((2, 2, 2, 2, TOK, HD), BF),
        ),
        in_specs=[anywhere] * 7,
        out_specs=(anywhere, anywhere),
        scratch_shapes=[
            vmem((4, 2, TOK, HD), BF),
            vmem((2, 2, 2, TOK, HD), BF),
            vmem((2, 2, 2, TOK, HD), BF),
            vmem((4, 2, ROWS, HD), BF),
            vmem((TOK, 512), BF),
            vmem((8, TOK, 512), BF),
            vmem((4, 4, 2, 128), F32),
            vmem((4, 2, 128), F32),
            vmem((256, 4096), BF),
            vmem((TOK, 2 * HD), BF),
            vmem((32, 128), jnp.int32),
            vmem((8, 128, 128), F32),
            vmem((2, 8, 512), F32),
            vmem((HD, 1024), BF),
            vmem((2, 1024, 512), F32),
            vmem((2, 8, 512), F32),
            vmem((2, 8, 512), F32),
            vmem((8, 512), F32),
            vmem((TOK, 2 * HD), BF),
            vmem((2, ROWS, HD), BF),
            vmem((1024, HD), F32),
            vmem((1024, HD), F32),
            vmem((HD, 512), F32),
            vmem((8, 512), F32),
            vmem((4, 2, TOK, HD), BF),
            vmem((2, 2, 2, 2, TOK, HD), BF),
            dma, dma, dma, dma, dma((3,)), dma((3,)),
            *query_sems, *key_sems, *key_sems, *query_sems, dma((8, 2)), dma((8, 2)), dma((4, 4)), dma((4, 4)),
            *query_sems, *key_sems,
        ],
        compiler_params=pltpu.CompilerParams(
            collective_id=0, has_side_effects=True, vmem_limit_bytes=60 * 1024 * 1024),
    )(queries, keys, values, attn_out, out_grad, out_weight, segment_ids.reshape(32, 128))
    return pl.pallas_call(
        deliver,
        out_shape=(out, out, out),
        in_specs=[pl.BlockSpec(memory_space=pltpu.VMEM)] * 2,
        out_specs=(pl.BlockSpec(memory_space=pltpu.VMEM),) * 3,
        name="deliver_call",
    )(*held)


def solution(mesh):
    return jax.shard_map(
        shards,
        mesh=mesh,
        in_specs=(
            P("seq", "head"),
            P("seq", "head"),
            P("seq", "head"),
            P("seq", "head"),
            P("seq", "head"),
            P("head", None),
            P(),
        ),
        out_specs=(P("seq", "head"), P("seq", "head"), P("seq", "head")),
        check_vma=False,
    )
```

time: 44.8 us -> 44.2 us (0.987)
  Pallas kernels: 44 us -> 43.4 us
    pallas_call x1, Pallas kernels: 42.4 us -> 41.5 us  [shards(): pl.pallas_call(kernel, out_shape=(jax.ShapeDtypeStruct((4, 2, TOK, HD), B...]
where the time goes in v4:
time: 44.2 us; the launch traced here: 44.1 us
  Pallas kernels  43.4 us (98%)
  between operations  0.64 us (1%)
    pallas_call x1, Pallas kernels, shards(): pl.pallas_call(kernel, out_shape=(jax.ShapeDtypeStruct((4, 2, TOK, HD), B...  41.5 us
    pallas_call x1, Pallas kernels, shards(): pl.pallas_call(deliver, out_shape=(out, out, out), in_specs=[pl.BlockSpec...  1.9 us

profile of v4, /device:TPU:1, one launch (start us, length us, event | category | flops | bytes accessed | tf_op | source)
XLA Modules:
  0.0 44.1 jit_solution(8749096581091112567)
XLA Ops:
  0.6 41.5 %shard_map.94 = (bf16[4,2,128,128]{3,2,1,0:T(8,128)(2,1)}, bf16[2,2,2,2,128,128]{5,4,3,2,1,0:T(8,128)(2,1)}) custom-call(bf16[128,256]{1,0:T(8,128)(2,1)} %q_hbm.1, bf16[128,256]{1,0:T(8,128)(2,1)} %k_hbm.1, bf16[128,256]{1,0:T(8,128)(2,1)} %v_hbm.1, bf16[128,256]{1,0:T(8,128)(2,1)} %o_hbm.1, bf16[128,512]{1,0:T(8,128)(2,1)} %og_hbm.1, ...), custom_call_target="tpu_custom_call" | custom-call | tf_op jit(solution)/shard_map/pallas_call | solution.py:438
  42.2 1.9 %deliver_call.1 = (bf16[128,256]{1,0:T(8,128)(2,1)}, bf16[128,256]{1,0:T(8,128)(2,1)}, bf16[128,256]{1,0:T(8,128)(2,1)}) custom-call(bf16[4,2,128,128]{3,2,1,0:T(8,128)(2,1)} %get-tuple-element.5.dq_in, bf16[2,2,2,2,128,128]{5,4,3,2,1,0:T(8,128)(2,1)} %get-tuple-element.6.dkv_in), custom_call_target="tpu_custom_call" | custom-call | tf_op jit(solution)/shard_map/deliver_call/pallas_call | solution.py:480

commit v5 on v4

--- a/solution.py
+++ b/solution.py
@@ -63,7 +63,7 @@
 def kernel(
     q_hbm, k_hbm, v_hbm, o_hbm, og_hbm, w_hbm, seg_hbm,
     dq_in, dkv_in,
-    qb, kb, vb, gb, og_own, ogb, ls_in, ls_out, w_ref, o_ref, seg_ref, segk, segq, kt, pb, mb, sh, lb, ga,
+    qb, kb, vb, gb, og_own, ogb, ls_in, ls_out, w_ref, o_ref, seg_ref, segk, segq, kt, pb, mb, sh, lb, acc, ga,
     gstage, dka, dva, dqt, dlt, dq_out, dkv_out,
     w_sem, o_sem, seg_sem, og_sem, own_sem, res_sem,
     q_s, q_r, k_s, k_r, v_s, v_r, g_s, g_r, og_s, og_r, ls_s, ls_r, dq_s, dq_r, dkv_s, dkv_r,
@@ -247,14 +247,6 @@
     scores(0, 0)
     rows_on_x()
     rows_on_y()
-    for cc in range(2):
-        arrived(kb, k_r, 1, 0, cc)
-        arrived(kb, k_r, 1, 1, cc)
-    scores(0, 1)
-    blocks_arrived(qb, q_r, 1)
-    scores(1, 0)
-    scores(1, 1)
-    keys_on(vb, v_s, v_r)
 
     def share_copy(d, e):
         return to_seq(ls_out.at[d], ls_in.at[e, d], ls_s.at[d, e], ls_r.at[e, d], device(0, SHARE_STEPS[d][e], 0))
@@ -283,21 +275,33 @@
                 if e != d:
                     go(share_copy(d, e))
 
+    def out_products(*slots):
+        total = None
+        for slot in slots:
+            block = heads_at[slot // 4, slot % 4]
+            for part in range(2):
+                if slot and (slot, part) not in ((4, 0), (1, 1), (2, 1), (3, 1)):
+                    rows_arrived(slot, part)
+            rows = ogb[slot] if slot else og_own[...]
+            term = dot_nt(rows, w_ref[:, pl.ds(pl.multiple_of(block * 512, 512), 512)])
+            total = term if total is None else total + term
+        return total
+
+    for cc in range(2):
+        arrived(kb, k_r, 1, 0, cc)
+        arrived(kb, k_r, 1, 1, cc)
+    scores(0, 1)
     sums(0)
+    blocks_arrived(qb, q_r, 1)
+    scores(1, 0)
+    scores(1, 1)
+
     sums(1)
+    keys_on(vb, v_s, v_r)
     for copy in local[3:]:
         copy.wait()
-
-    acc = None
-    for slot in (0, 4, 1, 3, 2, 5, 7, 6):
-        block = heads_at[slot // 4, slot % 4]
-        for part in range(2):
-            if slot and (slot, part) not in ((4, 0), (1, 1), (2, 1), (3, 1)):
-                rows_arrived(slot, part)
-        rows = ogb[slot] if slot else og_own[...]
-        term = dot_nt(rows, w_ref[:, pl.ds(pl.multiple_of(block * 512, 512), 512)])
-        acc = term if acc is None else acc + term
-    ga[...] = acc.astype(BF)
+    acc[...] = out_products(0, 4, 1, 3, 2)
+    ga[...] = (acc[...] + out_products(5, 7, 6)).astype(BF)
     for cc in range(2):
         grad = ga[:, cols(cc)]
         delta = jnp.sum((grad.astype(F32) * o_ref[:, cols(cc)].astype(F32)).T, axis=0, keepdims=True)
@@ -416,16 +420,26 @@
         copy.wait()
 
 
-def deliver(dq_in, dkv_in, dq_ref, dk_ref, dv_ref):
+def deliver(dq_in, dkv_in, dq_ref, dk_ref, dv_ref, dq_parts, key_parts, outs, in_sem, out_sem):
     c = lax.axis_index("seq") % 2
-    for cc in range(2):
-        h = (c + cc) % 2
-        cols = pl.ds(pl.multiple_of(h * HD, HD), HD)
-        parts = [dq_in[d, cc].astype(F32) for d in range(4)]
-        dq_ref[:, cols] = (((parts[0] + parts[1]) + (parts[2] + parts[3])) * SCALE).astype(BF)
-        for a, ref in enumerate((dk_ref, dv_ref)):
-            parts = [dkv_in[dy, dz, cc, a].astype(F32) for dy in range(2) for dz in range(2)]
-            ref[:, cols] = ((parts[0] + parts[1]) + (parts[2] + parts[3])).astype(BF)
+    reads = [pltpu.make_async_copy(dq_in, dq_parts, in_sem.at[0])]
+    reads += [pltpu.make_async_copy(dkv_in.at[:, :, :, a], key_parts.at[a], in_sem.at[1 + a]) for a in range(2)]
+    writes = [pltpu.make_async_copy(outs.at[n], ref, out_sem.at[n]) for n, ref in enumerate((dq_ref, dk_ref, dv_ref))]
+    for copy in reads:
+        copy.start()
+    for n in range(3):
+        reads[n].wait()
+        for cc in range(2):
+            h = (c + cc) % 2
+            if n:
+                parts = [key_parts[n - 1, dy, dz, cc].astype(F32) for dy in range(2) for dz in range(2)]
+            else:
+                parts = [dq_parts[d, cc].astype(F32) for d in range(4)]
+            total = (parts[0] + parts[1]) + (parts[2] + parts[3])
+            outs[n, :, pl.ds(pl.multiple_of(h * HD, HD), HD)] = (total if n else total * SCALE).astype(BF)
+        writes[n].start()
+    for copy in writes:
+        copy.wait()
 
 
 def shards(queries, keys, values, attn_out, out_grad, out_weight, segment_ids):
@@ -462,6 +476,7 @@
             vmem((2, 8, 512), F32),
             vmem((2, 8, 512), F32),
             vmem((8, 512), F32),
+            vmem((TOK, 2 * HD), F32),
             vmem((TOK, 2 * HD), BF),
             vmem((2, ROWS, HD), BF),
             vmem((1024, HD), F32),
@@ -480,8 +495,15 @@
     return pl.pallas_call(
         deliver,
         out_shape=(out, out, out),
-        in_specs=[pl.BlockSpec(memory_space=pltpu.VMEM)] * 2,
-        out_specs=(pl.BlockSpec(memory_space=pltpu.VMEM),) * 3,
+        in_specs=[anywhere] * 2,
+        out_specs=(anywhere, anywhere, anywhere),
+        scratch_shapes=[
+            vmem((4, 2, TOK, HD), BF),
+            vmem((2, 2, 2, 2, TOK, HD), BF),
+            vmem((3, TOK, 2 * HD), BF),
+            dma((3,)), dma((3,)),
+        ],
+        compiler_params=pltpu.CompilerParams(vmem_limit_bytes=60 * 1024 * 1024),
         name="deliver_call",
     )(*held)
 

time: 44.2 us -> 43.9 us (level)
  no operation moved by 1% of the time
where the time goes in v5:
time: 43.9 us; the launch traced here: 43.7 us
  Pallas kernels  43.1 us (98%)
  between operations  0.64 us (1%)
    pallas_call x1, Pallas kernels, shards(): pl.pallas_call(kernel, out_shape=(jax.ShapeDtypeStruct((4, 2, TOK, HD), B...  41.3 us
    pallas_call x1, Pallas kernels, shards(): pl.pallas_call(deliver, out_shape=(out, out, out), in_specs=[anywhere] *...  1.83 us

profile of v5, /device:TPU:1, one launch (start us, length us, event | category | flops | bytes accessed | tf_op | source)
XLA Modules:
  0.0 43.7 jit_solution(15559956127018786349)
XLA Ops:
  0.6 41.3 %shard_map.94 = (bf16[4,2,128,128]{3,2,1,0:T(8,128)(2,1)}, bf16[2,2,2,2,128,128]{5,4,3,2,1,0:T(8,128)(2,1)}) custom-call(bf16[128,256]{1,0:T(8,128)(2,1)} %q_hbm.1, bf16[128,256]{1,0:T(8,128)(2,1)} %k_hbm.1, bf16[128,256]{1,0:T(8,128)(2,1)} %v_hbm.1, bf16[128,256]{1,0:T(8,128)(2,1)} %o_hbm.1, bf16[128,512]{1,0:T(8,128)(2,1)} %og_hbm.1, ...), custom_call_target="tpu_custom_call" | custom-call | tf_op jit(solution)/shard_map/pallas_call | solution.py:452
  41.9 1.8 %deliver_call.1 = (bf16[128,256]{1,0:T(8,128)(2,1)}, bf16[128,256]{1,0:T(8,128)(2,1)}, bf16[128,256]{1,0:T(8,128)(2,1)}) custom-call(bf16[4,2,128,128]{3,2,1,0:T(8,128)(2,1)} %get-tuple-element.5.dq_in, bf16[2,2,2,2,128,128]{5,4,3,2,1,0:T(8,128)(2,1)} %get-tuple-element.6.dkv_in), custom_call_target="tpu_custom_call" | custom-call | tf_op jit(solution)/shard_map/deliver_call/pallas_call | solution.py:495

commit v6 on v5

--- a/solution.py
+++ b/solution.py
@@ -292,6 +292,8 @@
         arrived(kb, k_r, 1, 1, cc)
     scores(0, 1)
     sums(0)
+    for n, (dy, dz, cc) in enumerate(KEY_SLOTS):
+        kt[:, n * 128:(n + 1) * 128] = kb[dy, dz, cc].astype(F32).T.astype(BF)
     blocks_arrived(qb, q_r, 1)
     scores(1, 0)
     scores(1, 1)
@@ -318,8 +320,6 @@
     send_grad(1, 0)
     gb[0, 0] = gstage[0]
     send_grad(2, 3)
-    for n, (dy, dz, cc) in enumerate(KEY_SLOTS):
-        kt[:, n * 128:(n + 1) * 128] = kb[dy, dz, cc].astype(F32).T.astype(BF)
     dka[...] = jnp.zeros(dka.shape, F32)
     dva[...] = jnp.zeros(dva.shape, F32)
     keys_arrived(vb, v_r)

time: 43.9 us -> 43.9 us (level)
  no operation moved by 1% of the time
where the time goes in v6:
time: 43.9 us; the launch traced here: 43.7 us
  Pallas kernels  43.1 us (98%)
  between operations  0.64 us (1%)
    pallas_call x1, Pallas kernels, shards(): pl.pallas_call(kernel, out_shape=(jax.ShapeDtypeStruct((4, 2, TOK, HD), B...  41.3 us
    pallas_call x1, Pallas kernels, shards(): pl.pallas_call(deliver, out_shape=(out, out, out), in_specs=[anywhere] *...  1.83 us

profile of v6, /device:TPU:1, one launch (start us, length us, event | category | flops | bytes accessed | tf_op | source)
XLA Modules:
  0.0 43.7 jit_solution(15548759111912172241)
XLA Ops:
  0.6 41.3 %shard_map.94 = (bf16[4,2,128,128]{3,2,1,0:T(8,128)(2,1)}, bf16[2,2,2,2,128,128]{5,4,3,2,1,0:T(8,128)(2,1)}) custom-call(bf16[128,256]{1,0:T(8,128)(2,1)} %q_hbm.1, bf16[128,256]{1,0:T(8,128)(2,1)} %k_hbm.1, bf16[128,256]{1,0:T(8,128)(2,1)} %v_hbm.1, bf16[128,256]{1,0:T(8,128)(2,1)} %o_hbm.1, bf16[128,512]{1,0:T(8,128)(2,1)} %og_hbm.1, ...), custom_call_target="tpu_custom_call" | custom-call | tf_op jit(solution)/shard_map/pallas_call | solution.py:452
  41.9 1.8 %deliver_call.1 = (bf16[128,256]{1,0:T(8,128)(2,1)}, bf16[128,256]{1,0:T(8,128)(2,1)}, bf16[128,256]{1,0:T(8,128)(2,1)}) custom-call(bf16[4,2,128,128]{3,2,1,0:T(8,128)(2,1)} %get-tuple-element.5.dq_in, bf16[2,2,2,2,128,128]{5,4,3,2,1,0:T(8,128)(2,1)} %get-tuple-element.6.dkv_in), custom_call_target="tpu_custom_call" | custom-call | tf_op jit(solution)/shard_map/deliver_call/pallas_call | solution.py:495
